TPU v7x, 256 devices: a whole 4x4x8 slice. The times are simulated.
256 devices in a mesh: dp: 32 (over y, x, core), tensor: 8 (over z).
Axes of the slice: x: 4, y: 4, z: 8, core: 2. Of those that a mesh axis runs over, the one named last changes fastest.
Arguments:
- queries: bfloat16 [32768, 4096], P(('dp', 'tensor')), may hold values from -170 to 170
- keys: bfloat16 [32768, 1024], P(('dp', 'tensor')), may hold values from -7 to 7
- values: bfloat16 [32768, 1024], P(('dp', 'tensor')), may hold values from -6 to 6
- grad_out: bfloat16 [32768, 4096], P(('dp', 'tensor')), may hold values from -12 to 12
- chosen_len: int32 [128], replicated, may hold values from 16 to 240
- pack_of: int32 [128], replicated, may hold values from 0 to 31, as said below
- pack_offset: int32 [128], replicated, may hold values from 0 to 768, as said below
Outputs:
- grad_queries: bfloat16 [32768, 4096], P(('dp', 'tensor'))
- grad_keys: bfloat16 [32768, 1024], P(('dp', 'tensor'))
- grad_values: bfloat16 [32768, 1024], P(('dp', 'tensor'))
Inputs may be any that keep to these rules, and one draw needn't show every extreme that they name: `pack_of`: every pack receives exactly 4 pairs; the 4 consecutive pairs of one loader shard go to 4 different packs, one pair to each. `pack_offset`: within one pack the offsets of its pairs are the multiples of 256 below 1024, each once.
All inputs are finite; a program needn't handle non-finite values.
Results may differ from a plain program's by a relative error of at most 0.011.
Values may be sent and summed in bfloat16 or wider, within the bound.
No kernel may reach another device: no remote copies, remote signals or barrier semaphores. Data moves between devices by JAX's collectives and lax.ppermute only.
A program may use at most 128 MiB of HBM per device.

v0:
```python
import math

import jax
import jax.numpy as jnp
from jax import lax
from jax.sharding import PartitionSpec as P

HEAD_WIDTH = 128
PAIR_TOKENS = 256
QUERY_PER_KEY = 4


def cell_ranks(targets):
    per_shard = targets.shape[1]
    same_cell = targets[:, :, None] == targets[:, None, :]
    index_vec = jnp.arange(per_shard, dtype=jnp.int32)
    before = index_vec[None, :] < index_vec[:, None]
    return jnp.sum(same_cell & before[None], axis=2)


def send_layout(targets, ranks, shard_here, capacity):
    shards, per_shard = targets.shape
    own_targets = lax.dynamic_index_in_dim(targets, shard_here, 0, keepdims=False)
    own_ranks = lax.dynamic_index_in_dim(ranks, shard_here, 0, keepdims=False)
    slot_of = own_targets * capacity + own_ranks
    every_slot = jnp.arange(shards * capacity, dtype=jnp.int32)[:, None]
    matches = slot_of[None, :] == every_slot
    source_pair = jnp.sum(
        jnp.where(matches, jnp.arange(per_shard, dtype=jnp.int32)[None, :], 0), axis=1
    )
    occupied = jnp.any(matches, axis=1)
    return (source_pair, occupied)


def receive_layout(targets, ranks, pack_offset, chosen_len, shard_here, capacity):
    shards, per_shard = targets.shape
    slot_table = (pack_offset // PAIR_TOKENS).reshape(shards, per_shard)
    length_table = chosen_len.reshape(shards, per_shard)
    arrival = jnp.arange(shards, dtype=jnp.int32)[:, None] * capacity + ranks
    wanted = jnp.arange(per_shard, dtype=jnp.int32)[:, None, None]
    hits = (targets[None] == shard_here) & (slot_table[None] == wanted)
    arrival_index = jnp.sum(jnp.where(hits, arrival[None], 0), axis=(1, 2))
    arrival_length = jnp.sum(jnp.where(hits, length_table[None], 0), axis=(1, 2))
    return (arrival_index, arrival_length)


def pick_blocks(array, source_pair, occupied):
    columns = array.shape[-1]
    blocks = array.reshape(-1, PAIR_TOKENS, columns)
    picked = jnp.take(blocks, source_pair, axis=0)
    return jnp.where(occupied[:, None, None], picked, jnp.zeros_like(picked)).reshape(-1, columns)


def place_blocks(array, arrival_index):
    columns = array.shape[-1]
    blocks = array.reshape(-1, PAIR_TOKENS, columns)
    return jnp.take(blocks, arrival_index, axis=0)


def attend_single(query_part, grad_part, key_part, value_part, chosen):
    rows, query_cols = query_part.shape
    kv_local = key_part.shape[1] // HEAD_WIDTH
    scale = 1.0 / math.sqrt(HEAD_WIDTH)
    position = jnp.arange(rows, dtype=jnp.int32)
    segment = (position >= chosen).astype(jnp.int32)
    allowed = (segment[:, None] == segment[None, :]) & (position[None, :] <= position[:, None])
    query_four = query_part.reshape(rows, kv_local, QUERY_PER_KEY, HEAD_WIDTH)
    gradient_four = grad_part.reshape(rows, kv_local, QUERY_PER_KEY, HEAD_WIDTH)
    key_three = key_part.reshape(rows, kv_local, HEAD_WIDTH)
    value_three = value_part.reshape(rows, kv_local, HEAD_WIDTH)
    scores = (
        jnp.einsum("rhgd,shd->hgrs", query_four, key_three, preferred_element_type=jnp.float32)
        * scale
    )
    scores = jnp.where(allowed[None, None], scores, -jnp.inf)
    peak = jnp.max(scores, axis=-1, keepdims=True)
    weights = jnp.exp(scores - peak)
    probs = weights / jnp.sum(weights, axis=-1, keepdims=True)
    probs_b = probs.astype(jnp.bfloat16)
    attended = jnp.einsum(
        "hgrs,shd->rhgd", probs_b, value_three, preferred_element_type=jnp.float32
    )
    delta = jnp.sum(gradient_four.astype(jnp.float32) * attended, axis=-1)
    dprob = jnp.einsum(
        "rhgd,shd->hgrs", gradient_four, value_three, preferred_element_type=jnp.float32
    )
    dscore = probs * (dprob - jnp.transpose(delta, (1, 2, 0))[..., None])
    dscore_b = dscore.astype(jnp.bfloat16)
    pair_query_gradient = (
        jnp.einsum("hgrs,shd->rhgd", dscore_b, key_three, preferred_element_type=jnp.float32)
        * scale
    )
    pair_key_gradient = (
        jnp.einsum("hgrs,rhgd->shd", dscore_b, query_four, preferred_element_type=jnp.float32)
        * scale
    )
    pair_value_gradient = jnp.einsum(
        "hgrs,rhgd->shd", probs_b, gradient_four, preferred_element_type=jnp.float32
    )
    return (
        pair_query_gradient.reshape(rows, query_cols).astype(jnp.bfloat16),
        pair_key_gradient.reshape(rows, kv_local * HEAD_WIDTH).astype(jnp.bfloat16),
        pair_value_gradient.reshape(rows, kv_local * HEAD_WIDTH).astype(jnp.bfloat16),
    )


def attend(query_part, grad_part, key_part, value_part, chosen):

    def single(items):
        return attend_single(items[0], items[1], items[2], items[3], items[4])

    query_gradient, key_gradient, value_gradient = lax.map(
        single, (query_part, grad_part, key_part, value_part, chosen)
    )
    return (
        query_gradient.reshape(-1, query_gradient.shape[-1]),
        key_gradient.reshape(-1, key_gradient.shape[-1]),
        value_gradient.reshape(-1, value_gradient.shape[-1]),
    )


def per_device(queries, keys, values, grad_out, chosen_len, pack_of, pack_offset):
    tensor_count = lax.axis_size("tensor")
    shard_count = lax.axis_size("dp")
    shard_here = lax.axis_index("dp")
    per_shard = queries.shape[0] * tensor_count // PAIR_TOKENS
    capacity = (per_shard + shard_count - 1) // shard_count
    query_heads, grad_heads, key_heads, value_heads = (
        lax.all_to_all(queries, "tensor", split_axis=1, concat_axis=0, tiled=True),
        lax.all_to_all(grad_out, "tensor", split_axis=1, concat_axis=0, tiled=True),
        lax.all_to_all(keys, "tensor", split_axis=1, concat_axis=0, tiled=True),
        lax.all_to_all(values, "tensor", split_axis=1, concat_axis=0, tiled=True),
    )
    targets = pack_of.reshape(shard_count, per_shard)
    ranks = cell_ranks(targets)
    source_pair, occupied = send_layout(targets, ranks, shard_here, capacity)
    arrival_index, arrival_length = receive_layout(
        targets, ranks, pack_offset, chosen_len, shard_here, capacity
    )
    sent_query = pick_blocks(query_heads, source_pair, occupied)
    sent_grad = pick_blocks(grad_heads, source_pair, occupied)
    sent_key = pick_blocks(key_heads, source_pair, occupied)
    sent_value = pick_blocks(value_heads, source_pair, occupied)
    got_query, got_grad, got_key, got_value = (
        lax.all_to_all(sent_query, "dp", split_axis=0, concat_axis=0, tiled=True),
        lax.all_to_all(sent_grad, "dp", split_axis=0, concat_axis=0, tiled=True),
        lax.all_to_all(sent_key, "dp", split_axis=0, concat_axis=0, tiled=True),
        lax.all_to_all(sent_value, "dp", split_axis=0, concat_axis=0, tiled=True),
    )
    query_gradient, key_gradient, value_gradient = attend(
        place_blocks(got_query, arrival_index),
        place_blocks(got_grad, arrival_index),
        place_blocks(got_key, arrival_index),
        place_blocks(got_value, arrival_index),
        arrival_length,
    )
    out_q, out_k, out_v = (
        lax.all_to_all(query_gradient, "tensor", split_axis=0, concat_axis=1, tiled=True),
        lax.all_to_all(key_gradient, "tensor", split_axis=0, concat_axis=1, tiled=True),
        lax.all_to_all(value_gradient, "tensor", split_axis=0, concat_axis=1, tiled=True),
    )
    return (out_q, out_k, out_v)


def solution(mesh):
    return jax.shard_map(
        per_device,
        mesh=mesh,
        in_specs=(
            P(("dp", "tensor"), None),
            P(("dp", "tensor"), None),
            P(("dp", "tensor"), None),
            P(("dp", "tensor"), None),
            P(),
            P(),
            P(),
        ),
        out_specs=(P(("dp", "tensor"), None), P(("dp", "tensor"), None), P(("dp", "tensor"), None)),
        check_vma=False,
    )
```

profile of v0, /device:TPU:11, one launch (start us, length us, event | category | flops | bytes accessed | tf_op | source)
XLA Modules:
  0.0 476.3 jit_solution(13636327418450991801)
XLA Ops:
  0.6 1.9 copy.109
  2.5 8.2 %all-to-all-start.4 = ((bf16[128,8,128]{0,2,1:T(8,128)(2,1)}), bf16[128,8,128]{0,2,1:T(8,128)(2,1)S(1)}, u32[]{:S(2)}, u32[]{:S(2)}) async-start(bf16[128,8,128]{0,2,1:T(8,128)(2,1)} %bitcast.38), calls=%async_computation.4 | async-start | bytes 524288 | tf_op jit(solution)/shard_map/all_to_all | solution.py:132
  10.7 1.8 copy.104
  12.5 8.6 %all-to-all-done.4 = bf16[128,8,128]{0,2,1:T(8,128)(2,1)S(1)} async-done(((bf16[128,8,128]{0,2,1:T(8,128)(2,1)}), bf16[128,8,128]{0,2,1:T(8,128)(2,1)S(1)}, u32[]{:S(2)}, u32[]{:S(2)}) %all-to-all-start.4) | async-done | bytes 262176 | tf_op jit(solution)/shard_map/all_to_all | solution.py:132
  21.1 3.4 all-to-all-start
  24.5 2.3 copy.107
  26.8 7.1 %all-to-all-done = bf16[128,8,128]{0,2,1:T(8,128)(2,1)S(1)} async-done(((bf16[128,8,128]{0,2,1:T(8,128)(2,1)}), bf16[128,8,128]{0,2,1:T(8,128)(2,1)S(1)}, u32[]{:S(2)}, u32[]{:S(2)}) %all-to-all-start) | async-done | bytes 262176 | tf_op jit(solution)/shard_map/all_to_all | solution.py:131
  33.8 3.6 all-to-all-start.2
  37.4 1.3 copy.111
  38.7 24.8 %all-to-all-done.2 = bf16[128,8,512]{0,2,1:T(8,128)(2,1)S(1)} async-done(((bf16[128,8,512]{0,2,1:T(8,128)(2,1)}), bf16[128,8,512]{0,2,1:T(8,128)(2,1)S(1)}, u32[]{:S(2)}, u32[]{:S(2)}) %all-to-all-start.2) | async-done | bytes 1048608 | tf_op jit(solution)/shard_map/all_to_all | solution.py:129
  63.5 4.2 all-to-all-start.6
  68.9 1.0 gather_fusion.4
  69.8 2.1 gather_fusion
  71.9 4.1 select_select_fusion.2
  76.0 18.0 %all-to-all-done.6 = bf16[128,8,512]{0,2,1:T(8,128)(2,1)} async-done(((bf16[128,8,512]{0,2,1:T(8,128)(2,1)}), bf16[128,8,512]{0,2,1:T(8,128)(2,1)}, u32[]{:S(2)}, u32[]{:S(2)}) %all-to-all-start.6) | async-done | bytes 1048608 | tf_op jit(solution)/shard_map/all_to_all | solution.py:130
  94.0 10.7 %all-to-all-start.5 = ((bf16[32,256,128]{2,1,0:T(8,128)(2,1)}), bf16[32,256,128]{2,1,0:T(8,128)(2,1)}, u32[]{:S(2)}, u32[]{:S(2)}) async-start(bf16[32,256,128]{2,1,0:T(8,128)(2,1)} %get-tuple-element.130), calls=%async_computation.5 | async-start | bytes 4194304 | tf_op jit(solution)/shard_map/all_to_all | solution.py:148
  105.3 4.8 %gather_fusion.2 = bf16[32,256,512]{2,1,0:T(8,128)(2,1)} fusion(bf16[4,256,512]{2,1,0:T(8,128)(2,1)S(1)} %bitcast.170, s32[1024]{0:T(1024)S(1)} %pad_clamp_fusion.1), kind=kCustom, calls=%fused_computation.clone | custom fusion | bytes 16777344 | tf_op jit(solution)/shard_map/jit(_take)/gather | solution.py:50
  110.0 1.5 copy.112
  111.5 4.8 %gather_fusion.6 = bf16[32,256,512]{2,1,0:T(8,128)(2,1)} fusion(bf16[4,256,512]{2,1,0:T(8,128)(2,1)S(1)} %bitcast.169, s32[1024]{0:T(1024)S(1)} %pad_clamp_fusion.1), kind=kCustom, calls=%fused_computation.4.clone | custom fusion | bytes 16777344 | tf_op jit(solution)/shard_map/jit(_take)/gather | solution.py:50
  116.3 15.2 %all-to-all-done.5 = bf16[32,256,128]{2,1,0:T(8,128)(2,1)} async-done(((bf16[32,256,128]{2,1,0:T(8,128)(2,1)}), bf16[32,256,128]{2,1,0:T(8,128)(2,1)}, u32[]{:S(2)}, u32[]{:S(2)}) %all-to-all-start.5) | async-done | bytes 2097184 | tf_op jit(solution)/shard_map/all_to_all | solution.py:148
  131.5 7.2 %all-to-all-start.1 = ((bf16[32,256,128]{2,1,0:T(8,128)(2,1)}), bf16[32,256,128]{2,1,0:T(8,128)(2,1)S(1)}, u32[]{:S(2)}, u32[]{:S(2)}) async-start(bf16[32,256,128]{2,1,0:T(8,128)(2,1)} %get-tuple-element.131), calls=%async_computation.1 | async-start | bytes 4194304 | tf_op jit(solution)/shard_map/all_to_all | solution.py:147
  138.7 11.8 %select_select_fusion = (bf16[32,256,512]{2,1,0:T(8,128)(2,1)}, bf16[32,256,512]{2,1,0:T(8,128)(2,1)}) fusion(bf16[32,256,512]{2,1,0:T(8,128)(2,1)} %gather_fusion.6, pred[32]{0:T(512)(128)(4,1)S(1)} %compare_and_fusion.1, pred[32]{0:T(512)(128)(4,1)S(1)} %fusion.33, bf16[32,256,512]{2,1,0:T(8,128)(2,1)} %gather_fusion.2), kind=kLoop, calls=%fused_computation.54 | loop fusion | flops 16777216 | bytes 33554496 | tf_op jit(solution)/shard_map/jit(_where)/select_n | solution.py:51
  150.5 15.1 %all-to-all-done.1 = bf16[32,256,128]{2,1,0:T(8,128)(2,1)S(1)} async-done(((bf16[32,256,128]{2,1,0:T(8,128)(2,1)}), bf16[32,256,128]{2,1,0:T(8,128)(2,1)S(1)}, u32[]{:S(2)}, u32[]{:S(2)}) %all-to-all-start.1) | async-done | bytes 2097184 | tf_op jit(solution)/shard_map/all_to_all | solution.py:147
  165.5 102.1 %all_to_all.145 = bf16[32,256,512]{2,1,0:T(8,128)(2,1)} all-to-all(bf16[32,256,512]{2,1,0:T(8,128)(2,1)} %get-tuple-element.129), channel_id=1, replica_groups=mesh['dp'=32,'tensor'=8] {'dp'}, dimensions={0} | all-to-all | bytes 16777216 | tf_op jit(solution)/shard_map/all_to_all | solution.py:145
  267.7 8.0 %all-to-all-start.7 = ((bf16[32,256,512]{2,1,0:T(8,128)(2,1)}), bf16[32,256,512]{2,1,0:T(8,128)(2,1)}, u32[]{:S(2)}, u32[]{:S(2)}) async-start(bf16[32,256,512]{2,1,0:T(8,128)(2,1)} %get-tuple-element.128), calls=%async_computation.7 | async-start | bytes 16777216 | tf_op jit(solution)/shard_map/all_to_all | solution.py:146
  276.5 2.2 gather_fusion.5
  279.4 4.0 gather_fusion.3
  283.4 92.3 %all-to-all-done.7 = bf16[32,256,512]{2,1,0:T(8,128)(2,1)} async-done(((bf16[32,256,512]{2,1,0:T(8,128)(2,1)}), bf16[32,256,512]{2,1,0:T(8,128)(2,1)}, u32[]{:S(2)}, u32[]{:S(2)}) %all-to-all-start.7) | async-done | bytes 8388640 | tf_op jit(solution)/shard_map/all_to_all | solution.py:146
  375.7 4.0 gather_fusion.7
  379.7 1.6 broadcast_select_fusion
  381.3 29.9 %while.14 = (s32[]{:T(128)}, bf16[4,256,512]{2,1,0:T(8,128)(2,1)}, bf16[4,256,128]{2,1,0:T(8,128)(2,1)S(1)}, bf16[4,256,128]{2,1,0:T(8,128)(2,1)}, bf16[4,256,12...) while((s32[]{:T(128)}, bf16[4,256,512]{2,1,0:T(8,128)(2,1)}, ...), condition=%wide.region_9.14_spmd, body=%wide.region_5.13_spmd.sunk | while | flops 407008768 | bytes 13147277 | solution.py:112
  381.3 1.0 constant_dynamic-slice_fusion.5
  384.5 1.0 constant_dynamic-slice_fusion.4
  388.1 0.7 constant_dynamic-update-slice_fusion.5
  388.8 1.0 constant_dynamic-slice_fusion.5
  391.9 1.0 constant_dynamic-slice_fusion.4
  395.6 0.7 constant_dynamic-update-slice_fusion.5
  396.3 1.0 constant_dynamic-slice_fusion.5
  399.4 1.0 constant_dynamic-slice_fusion.4
  403.8 1.0 constant_dynamic-slice_fusion.5
  406.9 1.0 constant_dynamic-slice_fusion.4
  411.3 14.7 %all_to_all.146 = bf16[8,128,128]{2,1,0:T(8,128)(2,1)S(1)} all-to-all(bf16[8,128,128]{2,1,0:T(8,128)(2,1)S(1)} %bitcast.189), channel_id=1, replica_groups=mesh['dp'=32,'tensor'=8] {'tensor'}, dimensions={0} | all-to-all | bytes 524288 | tf_op jit(solution)/shard_map/all_to_all | solution.py:159
  425.9 15.6 %all_to_all.147 = bf16[8,128,128]{2,1,0:T(8,128)(2,1)S(1)} all-to-all(bf16[8,128,128]{2,1,0:T(8,128)(2,1)} %bitcast.190), channel_id=1, replica_groups=mesh['dp'=32,'tensor'=8] {'tensor'}, dimensions={0} | all-to-all | bytes 524288 | tf_op jit(solution)/shard_map/all_to_all | solution.py:160
  441.6 3.6 all-to-all-start.8
  445.3 0.9 copy.122
  446.4 0.9 copy.123
  447.2 27.1 %all-to-all-done.8 = bf16[8,128,512]{2,1,0:T(8,128)(2,1)S(1)} async-done(((bf16[8,128,512]{2,1,0:T(8,128)(2,1)}), bf16[8,128,512]{2,1,0:T(8,128)(2,1)S(1)}, u32[]{:S(2)}, u32[]{:S(2)}) %all-to-all-start.8) | async-done | bytes 1048608 | tf_op jit(solution)/shard_map/all_to_all | solution.py:158
  475.0 1.3 copy.121
  (115 shorter events, 24.4 us)
Async XLA Ops:
  0.6 36.8 %copy-start.2 = (bf16[128,4096]{1,0:T(8,128)(2,1)S(1)}, bf16[128,4096]{1,0:T(8,128)(2,1)}, u32[]{:S(2)}) copy-start(bf16[128,4096]{1,0:T(8,128)(2,1)} %param.20) | copy-start | bytes 3145732
  2.5 18.6 %all-to-all-start.4 = ((bf16[128,8,128]{0,2,1:T(8,128)(2,1)}), bf16[128,8,128]{0,2,1:T(8,128)(2,1)S(1)}, u32[]{:S(2)}, u32[]{:S(2)}) async-start(bf16[128,8,128]{0,2,1:T(8,128)(2,1)} %bitcast.38), calls=%async_computation.4 | async-start | bytes 524288 | tf_op jit(solution)/shard_map/all_to_all | solution.py:132
  21.1 12.8 %all-to-all-start = ((bf16[128,8,128]{0,2,1:T(8,128)(2,1)}), bf16[128,8,128]{0,2,1:T(8,128)(2,1)S(1)}, u32[]{:S(2)}, u32[]{:S(2)}) async-start(bf16[128,8,128]{0,2,1:T(8,128)(2,1)} %bitcast.32), calls=%async_computation | async-start | bytes 524288 | tf_op jit(solution)/shard_map/all_to_all | solution.py:131
  24.5 43.3 %copy-start.3 = (s32[128]{0:T(128)S(1)}, s32[128]{0:T(128)}, u32[]{:S(2)}) copy-start(s32[128]{0:T(128)} %param.22) | copy-start | bytes 1540
  33.8 29.7 %all-to-all-start.2 = ((bf16[128,8,512]{0,2,1:T(8,128)(2,1)}), bf16[128,8,512]{0,2,1:T(8,128)(2,1)S(1)}, u32[]{:S(2)}, u32[]{:S(2)}) async-start(bf16[128,8,512]{0,2,1:T(8,128)(2,1)} %bitcast.35), calls=%async_computation.2 | async-start | bytes 2097152 | tf_op jit(solution)/shard_map/all_to_all | solution.py:129
  63.5 4.9 %copy-start = (bf16[128,8,512]{0,2,1:T(8,128)(2,1)}, bf16[128,8,512]{0,2,1:T(8,128)(2,1)S(1)}, u32[]{:S(2)}) copy-start(bf16[128,8,512]{0,2,1:T(8,128)(2,1)S(1)} %all-to-all-done.2) | copy-start | bytes 3145732
  63.5 30.4 %all-to-all-start.6 = ((bf16[128,8,512]{0,2,1:T(8,128)(2,1)}), bf16[128,8,512]{0,2,1:T(8,128)(2,1)}, u32[]{:S(2)}, u32[]{:S(2)}) async-start(bf16[128,8,512]{0,2,1:T(8,128)(2,1)} %bitcast.41), calls=%async_computation.6 | async-start | bytes 2097152 | tf_op jit(solution)/shard_map/all_to_all | solution.py:130
  76.0 28.7 %copy-start.1 = (bf16[128,8,512]{0,2,1:T(8,128)(2,1)S(1)}, bf16[128,8,512]{0,2,1:T(8,128)(2,1)}, u32[]{:S(2)}) copy-start(bf16[128,8,512]{0,2,1:T(8,128)(2,1)} %copy-done) | copy-start | bytes 3145732
  94.0 37.6 %all-to-all-start.5 = ((bf16[32,256,128]{2,1,0:T(8,128)(2,1)}), bf16[32,256,128]{2,1,0:T(8,128)(2,1)}, u32[]{:S(2)}, u32[]{:S(2)}) async-start(bf16[32,256,128]{2,1,0:T(8,128)(2,1)} %get-tuple-element.130), calls=%async_computation.5 | async-start | bytes 4194304 | tf_op jit(solution)/shard_map/all_to_all | solution.py:148
  131.5 34.0 %all-to-all-start.1 = ((bf16[32,256,128]{2,1,0:T(8,128)(2,1)}), bf16[32,256,128]{2,1,0:T(8,128)(2,1)S(1)}, u32[]{:S(2)}, u32[]{:S(2)}) async-start(bf16[32,256,128]{2,1,0:T(8,128)(2,1)} %get-tuple-element.131), calls=%async_computation.1 | async-start | bytes 4194304 | tf_op jit(solution)/shard_map/all_to_all | solution.py:147
  267.7 8.1 %copy-start.5 = (s32[128]{0:T(128)S(1)}, s32[128]{0:T(128)}, u32[]{:S(2)}) copy-start(s32[128]{0:T(128)} %param.23) | copy-start | bytes 1540
  267.7 8.3 %copy-start.4 = (s32[128]{0:T(128)S(1)}, s32[128]{0:T(128)}, u32[]{:S(2)}) copy-start(s32[128]{0:T(128)} %param.21) | copy-start | bytes 1540
  267.7 108.1 %all-to-all-start.7 = ((bf16[32,256,512]{2,1,0:T(8,128)(2,1)}), bf16[32,256,512]{2,1,0:T(8,128)(2,1)}, u32[]{:S(2)}, u32[]{:S(2)}) async-start(bf16[32,256,512]{2,1,0:T(8,128)(2,1)} %get-tuple-element.128), calls=%async_computation.7 | async-start | bytes 16777216 | tf_op jit(solution)/shard_map/all_to_all | solution.py:146
  441.6 32.7 %all-to-all-start.8 = ((bf16[8,128,512]{2,1,0:T(8,128)(2,1)}), bf16[8,128,512]{2,1,0:T(8,128)(2,1)S(1)}, u32[]{:S(2)}, u32[]{:S(2)}) async-start(bf16[8,128,512]{2,1,0:T(8,128)(2,1)} %bitcast.182), calls=%async_computation.8 | async-start | bytes 2097152 | tf_op jit(solution)/shard_map/all_to_all | solution.py:158
where the time goes:
time: 478 us; the launch traced here: 476 us
  waiting for transfers between devices  208 us (44%)
  blocking collectives  132 us (28%)
  local copies, waits for them, and re-layouts  56 us (12%)
  starting transfers between devices  48.8 us (10%)
  other arithmetic  22.5 us (5%)
  matrix products  7.02 us (1%)
    all_to_all x1, blocking collectives, per_device(): lax.all_to_all(sent_query, 'dp', split_axis=0, concat_axis=0, tiled=True)  102 us
    all_to_all x1, waiting for transfers between devices, per_device(): lax.all_to_all(sent_grad, 'dp', split_axis=0, concat_axis=0, tiled=True)  92.3 us
    all_to_all x1, waiting for transfers between devices, per_device(): lax.all_to_all(query_gradient, 'tensor', split_axis=0, concat_axis=1, til...  27.1 us
    all_to_all x1, waiting for transfers between devices, per_device(): lax.all_to_all(queries, 'tensor', split_axis=1, concat_axis=0, tiled=True)  24.8 us
    all_to_all x1, waiting for transfers between devices, per_device(): lax.all_to_all(grad_out, 'tensor', split_axis=1, concat_axis=0, tiled=True)  18 us
    select_n x2, other arithmetic, pick_blocks(): jnp.where(occupied[:, None, None], picked, jnp.zeros_like(picked))  15.8 us
    all_to_all x1, blocking collectives, per_device(): lax.all_to_all(value_gradient, 'tensor', split_axis=0, concat_axis=1, til...  15.6 us
    all_to_all x1, waiting for transfers between devices, per_device(): lax.all_to_all(sent_value, 'dp', split_axis=0, concat_axis=0, tiled=True)  15.2 us
  transfers between devices with their start and end apart: 8, of which 8 were waited for; matrix products, arithmetic and copies ran while one was open for 10% of the time, Pallas kernels for 0%

commit v1 on v0

v1 whole, which is shorter than its diff:
```python
import functools
import math

import jax
import jax.numpy as jnp
from jax import lax
from jax.experimental import pallas as pl
from jax.experimental.pallas import tpu as pltpu
from jax.sharding import PartitionSpec as P

WIDTH = 128
PAIR = 256
HALF = 128
GROUP = 4
BOTH = ("dp", "tensor")
CONTRACT_LAST = (((1,), (1,)), ((), ()))
CONTRACT_FIRST = (((0,), (0,)), ((), ()))


def attention_kernel(info, q_ref, g_ref, k_ref, v_ref, kp_ref, vp_ref, x_ref, own_ref, part_ref):
    chosen = info[0]
    second = info[1]
    scale = 1.0 / math.sqrt(WIDTH)
    f32 = jnp.float32
    bf16 = jnp.bfloat16

    row = lax.broadcasted_iota(jnp.int32, (HALF, PAIR), 0) + HALF * second
    col = lax.broadcasted_iota(jnp.int32, (HALF, PAIR), 1) - HALF * (1 - second)
    low = jnp.where(row >= chosen, chosen, 0)
    allowed = (col >= low) & (col <= row)

    q4 = jnp.concatenate([q_ref[:, i * WIDTH : (i + 1) * WIDTH] for i in range(GROUP)], axis=0)
    g4 = jnp.concatenate([g_ref[:, i * WIDTH : (i + 1) * WIDTH] for i in range(GROUP)], axis=0)
    kc = jnp.concatenate([kp_ref[...], k_ref[...]], axis=0)
    vc = jnp.concatenate([vp_ref[...], v_ref[...]], axis=0)

    scores = lax.dot_general(q4, kc, CONTRACT_LAST, preferred_element_type=f32) * scale
    dprob = lax.dot_general(g4, vc, CONTRACT_LAST, preferred_element_type=f32)
    scores = jnp.where(allowed[None], scores.reshape(GROUP, HALF, PAIR), -1e30).reshape(GROUP * HALF, PAIR)
    peak = jnp.max(scores, axis=1, keepdims=True)
    weights = jnp.exp(scores - peak)
    probs = weights * (1.0 / jnp.sum(weights, axis=1, keepdims=True))
    probs_b = probs.astype(bf16)
    delta = jnp.sum(probs_b.astype(f32) * dprob, axis=1, keepdims=True)
    dscore_b = (probs * (dprob - delta)).astype(bf16)
    dq = lax.dot_general(dscore_b, kc, (((1,), (0,)), ((), ())), preferred_element_type=f32) * scale
    dk = lax.dot_general(dscore_b, q4, CONTRACT_FIRST, preferred_element_type=f32) * scale
    dv = lax.dot_general(probs_b, g4, CONTRACT_FIRST, preferred_element_type=f32)

    def tiles(block):
        return block.reshape(HALF // 8, 8, WIDTH)

    for i in range(GROUP):
        x_ref[:, i // 2, :, (i % 2) * WIDTH : (i % 2 + 1) * WIDTH] = tiles(dq[i * HALF : (i + 1) * HALF]).astype(bf16)
    own_ref[:, 0] = tiles(dk[HALF:])
    own_ref[:, 1] = tiles(dv[HALF:])
    part_ref[:, 0] = tiles(dk[:HALF]).astype(bf16)
    part_ref[:, 1] = tiles(dv[:HALF]).astype(bf16)


def attention(info, q, g, k, v, kp, vp):
    heads = k.shape[1] // WIDTH
    groups = HALF // 8
    narrow = pl.BlockSpec((HALF, WIDTH), lambda h, info: (0, h))
    wide = pl.BlockSpec((HALF, GROUP * WIDTH), lambda h, info: (0, h))
    small = pl.BlockSpec((groups, 2, 8, WIDTH), lambda h, info: (0, h, 0, 0))
    return pl.pallas_call(
        attention_kernel,
        grid_spec=pltpu.PrefetchScalarGridSpec(
            num_scalar_prefetch=1,
            grid=(heads,),
            in_specs=[wide, wide, narrow, narrow, narrow, narrow],
            out_specs=[pl.BlockSpec((groups, 2, 8, 3 * WIDTH), lambda h, info: (0, h, 0, 0)), small, small],
        ),
        out_shape=[
            jax.ShapeDtypeStruct((groups, 2 * heads, 8, 3 * WIDTH), jnp.bfloat16),
            jax.ShapeDtypeStruct((groups, 2 * heads, 8, WIDTH), jnp.float32),
            jax.ShapeDtypeStruct((groups, 2 * heads, 8, WIDTH), jnp.bfloat16),
        ],
        compiler_params=pltpu.CompilerParams(vmem_limit_bytes=32 * 1024 * 1024),
        name="attention",
    )(info, q, g, k, v, kp, vp)


def combine_kernel(own_ref, part_ref, x_in, x_ref):
    del x_in
    x_ref[...] = (own_ref[...] + part_ref[...].astype(jnp.float32)).astype(jnp.bfloat16)


def combine(own, part, x):
    whole = pl.BlockSpec(own.shape, lambda i: (0, 0, 0, 0))
    return pl.pallas_call(
        combine_kernel,
        grid=(1,),
        in_specs=[whole, whole, pl.BlockSpec(memory_space=pl.ANY)],
        out_specs=pl.BlockSpec(own.shape, lambda i: (0, 0, 0, 2)),
        out_shape=jax.ShapeDtypeStruct(x.shape, x.dtype),
        input_output_aliases={2: 0},
        compiler_params=pltpu.CompilerParams(vmem_limit_bytes=32 * 1024 * 1024),
        name="combine",
    )(own, part, x)


def reorder_kernel(pack_of, pack_offset, y_ref, x_ref, sem):
    pairs = y_ref.shape[0]

    def step(i, carry):
        block = pack_of[i] * (1024 // PAIR) + pack_offset[i] // PAIR
        pltpu.make_async_copy(y_ref.at[i], x_ref.at[block], sem).start()
        return carry

    lax.fori_loop(0, pairs, step, 0)
    pltpu.make_async_copy(y_ref, x_ref, sem).wait()


def reorder(pack_of, pack_offset, y):
    return pl.pallas_call(
        reorder_kernel,
        grid_spec=pltpu.PrefetchScalarGridSpec(
            num_scalar_prefetch=2,
            grid=(1,),
            in_specs=[pl.BlockSpec(memory_space=pl.ANY)],
            out_specs=pl.BlockSpec(memory_space=pl.ANY),
            scratch_shapes=[pltpu.SemaphoreType.DMA],
        ),
        out_shape=jax.ShapeDtypeStruct(y.shape, y.dtype),
        name="reorder",
    )(pack_of, pack_offset, y)


def place_kernel(z_ref, q_ref, k_ref, v_ref):
    def rows(block):
        return block.astype(jnp.float32).reshape(HALF, block.shape[-1]).astype(jnp.bfloat16)

    q_ref[:, : 2 * WIDTH] = rows(z_ref[:, 0, :, : 2 * WIDTH])
    q_ref[:, 2 * WIDTH :] = rows(z_ref[:, 1, :, : 2 * WIDTH])
    k_ref[...] = rows(z_ref[:, 0, :, 2 * WIDTH :])
    v_ref[...] = rows(z_ref[:, 1, :, 2 * WIDTH :])


def place(z):
    groups, double, _, _ = z.shape
    heads = double // 2
    narrow = pl.BlockSpec((HALF, WIDTH), lambda h: (0, h))
    return pl.pallas_call(
        place_kernel,
        grid=(heads,),
        in_specs=[pl.BlockSpec((groups, 2, 8, 3 * WIDTH), lambda h: (0, h, 0, 0))],
        out_specs=[pl.BlockSpec((HALF, GROUP * WIDTH), lambda h: (0, h)), narrow, narrow],
        out_shape=[
            jax.ShapeDtypeStruct((HALF, heads * GROUP * WIDTH), jnp.bfloat16),
            jax.ShapeDtypeStruct((HALF, heads * WIDTH), jnp.bfloat16),
            jax.ShapeDtypeStruct((HALF, heads * WIDTH), jnp.bfloat16),
        ],
        compiler_params=pltpu.CompilerParams(vmem_limit_bytes=32 * 1024 * 1024),
        name="place",
    )(z)


def per_device(queries, keys, values, grad_out, chosen_len, pack_of, pack_offset):
    tensor_count = lax.axis_size("tensor")
    devices = tensor_count * lax.axis_size("dp")
    tensor_here = lax.axis_index("tensor")
    device_here = lax.axis_index("dp") * tensor_count + tensor_here
    info = jnp.stack([chosen_len[device_here // 2], tensor_here % 2]).astype(jnp.int32)

    up = [(i, i + 1) for i in range(0, tensor_count, 2)]
    down = [(i + 1, i) for i in range(0, tensor_count, 2)]
    first_keys = lax.ppermute(keys, "tensor", up)
    first_values = lax.ppermute(values, "tensor", up)
    pieces, own, part = attention(info, queries, grad_out, keys, values, first_keys, first_values)
    part = lax.ppermute(part, "tensor", down)
    pieces = combine(own, part, pieces)
    shape = pieces.shape
    spread = lax.all_to_all(pieces.reshape(devices, 8, 3 * WIDTH), BOTH, split_axis=0, concat_axis=0, tiled=True)
    ordered = reorder(pack_of, pack_offset, spread.reshape(devices // 2, 2, 8, 3 * WIDTH))
    gathered = lax.all_to_all(ordered.reshape(devices, 8, 3 * WIDTH), BOTH, split_axis=0, concat_axis=0, tiled=True)
    return tuple(place(gathered.reshape(shape)))


def solution(mesh):
    rows = P(BOTH, None)
    return jax.shard_map(
        per_device,
        mesh=mesh,
        in_specs=(rows, rows, rows, rows, P(), P(), P()),
        out_specs=(rows, rows, rows),
        check_vma=False,
    )
```

time: 478 us -> 204 us (0.43)
  the two profiles are of different devices: /device:TPU:11 before, /device:TPU:1 now
where the time goes in v1:
time: 204 us
  blocking collectives  108 us (53%)
  Pallas kernels  61.2 us (30%)
  waiting for transfers between devices  20.1 us (10%)
  starting transfers between devices  6.99 us (3%)
  local copies, waits for them, and re-layouts  5.59 us (3%)
    all_to_all x1, blocking collectives, per_device(): lax.all_to_all(pieces.reshape(devices, 8, 3 * WIDTH), BOTH, split_axis=0,...  58.6 us
    all_to_all x1, blocking collectives, per_device(): lax.all_to_all(ordered.reshape(devices, 8, 3 * WIDTH), BOTH, split_axis=0...  49.8 us
    pallas_call x1, Pallas kernels, reorder(): pl.pallas_call(reorder_kernel, grid_spec=pltpu.PrefetchScalarGridSpec(num...  49.5 us
    ppermute x1, waiting for transfers between devices, per_device(): part = lax.ppermute(part, 'tensor', down)  12.5 us
    pallas_call x1, Pallas kernels, attention(): pl.pallas_call(attention_kernel, grid_spec=pltpu.PrefetchScalarGridSpec(n...  8.51 us
    ppermute x1, waiting for transfers between devices, per_device(): first_values = lax.ppermute(values, 'tensor', up)  5.62 us
    ppermute x1, starting transfers between devices, per_device(): first_keys = lax.ppermute(keys, 'tensor', up)  4.39 us
    unnamed x8, local copies, waits for them, and re-layouts  4.35 us
  transfers between devices with their start and end apart: 3, of which 3 were waited for; matrix products, arithmetic and copies ran while one was open for 1% of the time, Pallas kernels for 0%

profile of v1, /device:TPU:1, one launch (start us, length us, event | category | flops | bytes accessed | tf_op | source)
XLA Modules:
  0.0 203.7 jit_solution(7880723566038928092)
XLA Ops:
  0.6 4.4 %collective-permute-start = (bf16[128,1024]{1,0:T(8,128)(2,1)}, bf16[128,1024]{1,0:T(8,128)(2,1)S(1)}, u32[]{:S(2)}, u32[]{:S(2)}) collective-permute-start(bf16[128,1024]{1,0:T(8,128)(2,1)} %k_ref.1), channel_id=1, source_target_pairs={{0,1},{2,3},{4,5},{6,7},{8,9},{10,11},{12,13},{14,15},{16,17},{18,... | collective-permute-start | bytes 786440 | tf_op jit(solution)/shard_map/ppermute | solution.py:169
  5.0 1.3 collective-permute-start.1
  6.4 1.2 dynamic_slice.3
  7.6 0.7 pad_add_fusion.info
  8.3 2.0 collective-permute-done.kp_ref
  10.3 5.6 %collective-permute-done.1.vp_ref = bf16[128,1024]{1,0:T(8,128)(2,1)S(1)} collective-permute-done((bf16[128,1024]{1,0:T(8,128)(2,1)}, bf16[128,1024]{1,0:T(8,128)(2,1)S(1)}, u32[]{:S(2)}, u32[]{:S(2)}) %collective-permute-start.1) | collective-permute-done | bytes 262176 | tf_op jit(solution)/shard_map/ppermute | solution.py:170
  15.9 0.0 copy-start
  15.9 1.2 copy-done
  17.1 0.0 copy-start.1
  17.1 1.2 copy-done.1
  18.4 0.0 copy-start.2
  18.4 0.9 copy-done.2
  19.3 0.0 copy-start.3
  19.3 0.9 copy-done.3
  20.3 8.5 %attention.1 = (bf16[16,16,8,384]{3,2,1,0:T(8,128)(2,1)S(1)}, f32[16,16,8,128]{3,2,1,0:T(8,128)S(1)}, bf16[16,16,8,128]{3,2,1,0:T(8,128)(2,1)S(1)}) custom-call(s32[2]{0:T(128)S(1)} %pad_add_fusion.info, bf16[128,4096]{1,0:T(8,128)(2,1)S(1)} %copy-done, bf16[128,4096]{1,0:T(8,128)(2,1)S(1)} %copy-done.1, bf16[128,1024]{1,0:T(8,128)(2,1)S(1)} %copy-done.2, ...), custom_call_target="tpu_custom_call" | custom-call | tf_op jit(solution)/shard_map/attention/pallas_call | solution.py:67
  28.8 1.3 collective-permute-start.2
  30.1 12.5 %collective-permute-done.2.part_ref = bf16[16,16,8,128]{3,2,1,0:T(8,128)(2,1)S(1)} collective-permute-done((bf16[16,16,8,128]{3,2,1,0:T(8,128)(2,1)S(1)}, bf16[16,16,8,128]{3,2,1,0:T(8,128)(2,1)S(1)}, u32[]{:S(2)}, u32[]{:S(2)}) %collective-permute-start.2) | collective-permute-done | bytes 524320 | tf_op jit(solution)/shard_map/ppermute | solution.py:172
  42.6 0.3 combine.1
  42.8 58.6 %all_to_all.10 = bf16[256,8,384]{2,1,0:T(8,128)(2,1)} all-to-all(bf16[256,8,384]{2,1,0:T(8,128)(2,1)S(1)} %bitcast.6), channel_id=1, replica_groups=mesh['dp'=32,'tensor'=8] {'dp','tensor'}, dimensions={0} | all-to-all | bytes 3145728 | tf_op jit(solution)/shard_map/all_to_all | solution.py:175
  101.5 49.5 %reorder.1 = bf16[128,2,8,384]{3,2,1,0:T(8,128)(2,1)} custom-call(s32[128]{0:T(128)} %pack_of.1, s32[128]{0:T(128)} %pack_offset.1, bf16[128,2,8,384]{3,2,1,0:T(8,128)(2,1)} %bitcast.7), custom_call_target="tpu_custom_call" | custom-call | tf_op jit(solution)/shard_map/reorder/pallas_call | solution.py:117
  151.0 49.8 %all_to_all.11 = bf16[256,8,384]{2,1,0:T(8,128)(2,1)S(1)} all-to-all(bf16[256,8,384]{2,1,0:T(8,128)(2,1)} %bitcast.8), channel_id=1, replica_groups=mesh['dp'=32,'tensor'=8] {'dp','tensor'}, dimensions={0} | all-to-all | bytes 3145728 | tf_op jit(solution)/shard_map/all_to_all | solution.py:177
  200.8 2.9 %place.1 = (bf16[128,4096]{1,0:T(8,128)(2,1)}, bf16[128,1024]{1,0:T(8,128)(2,1)}, bf16[128,1024]{1,0:T(8,128)(2,1)}) custom-call(bf16[16,16,8,384]{3,2,1,0:T(8,128)(2,1)S(1)} %bitcast.5), custom_call_target="tpu_custom_call" | custom-call | tf_op jit(solution)/shard_map/place/pallas_call | solution.py:145
Async XLA Ops:
  0.6 9.7 %collective-permute-start = (bf16[128,1024]{1,0:T(8,128)(2,1)}, bf16[128,1024]{1,0:T(8,128)(2,1)S(1)}, u32[]{:S(2)}, u32[]{:S(2)}) collective-permute-start(bf16[128,1024]{1,0:T(8,128)(2,1)} %k_ref.1), channel_id=1, source_target_pairs={{0,1},{2,3},{4,5},{6,7},{8,9},{10,11},{12,13},{14,15},{16,17},{18,... | collective-permute-start | bytes 786440 | tf_op jit(solution)/shard_map/ppermute | solution.py:169
  5.0 10.9 %collective-permute-start.1 = (bf16[128,1024]{1,0:T(8,128)(2,1)}, bf16[128,1024]{1,0:T(8,128)(2,1)S(1)}, u32[]{:S(2)}, u32[]{:S(2)}) collective-permute-start(bf16[128,1024]{1,0:T(8,128)(2,1)} %v_ref.1), channel_id=1, source_target_pairs={{0,1},{2,3},{4,5},{6,7},{8,9},{10,11},{12,13},{14,15},{16,17},{18,... | collective-permute-start | bytes 786440 | tf_op jit(solution)/shard_map/ppermute | solution.py:170
  15.9 1.2 copy-start
  17.1 1.2 copy-start.1
  18.4 0.9 copy-start.2
  19.3 0.9 copy-start.3
  28.8 13.8 %collective-permute-start.2 = (bf16[16,16,8,128]{3,2,1,0:T(8,128)(2,1)S(1)}, bf16[16,16,8,128]{3,2,1,0:T(8,128)(2,1)S(1)}, u32[]{:S(2)}, u32[]{:S(2)}) collective-permute-start(bf16[16,16,8,128]{3,2,1,0:T(8,128)(2,1)S(1)} %get-tuple-element.7), channel_id=1, source_target_pairs={{1,0},{3,2},{5,4},{7,6},{9,8},{11,10},{13,12},{15,14},{17,16},{19,... | collective-permute-start | bytes 1572872 | tf_op jit(solution)/shard_map/ppermute | solution.py:172

commit v2 on v1

--- a/solution.py
+++ b/solution.py
@@ -12,6 +12,8 @@
 PAIR = 256
 HALF = 128
 GROUP = 4
+CHUNKS = 2
+VMEM_ATT = 32
 BOTH = ("dp", "tensor")
 CONTRACT_LAST = (((1,), (1,)), ((), ()))
 CONTRACT_FIRST = (((0,), (0,)), ((), ()))
@@ -58,72 +60,84 @@
     part_ref[:, 1] = tiles(dv[:HALF]).astype(bf16)
 
 
-def attention(info, q, g, k, v, kp, vp):
-    heads = k.shape[1] // WIDTH
+def attention(info, q, g, k, v, first, chunk, chunks, x=None):
+    all_heads = k.shape[1] // WIDTH
+    heads = all_heads // chunks
+    base = chunk * heads
     groups = HALF // 8
-    narrow = pl.BlockSpec((HALF, WIDTH), lambda h, info: (0, h))
-    wide = pl.BlockSpec((HALF, GROUP * WIDTH), lambda h, info: (0, h))
+    narrow = pl.BlockSpec((HALF, WIDTH), lambda h, info: (0, base + h))
+    wide = pl.BlockSpec((HALF, GROUP * WIDTH), lambda h, info: (0, base + h))
+    first_key = pl.BlockSpec((HALF, WIDTH), lambda h, info: (0, h))
+    first_value = pl.BlockSpec((HALF, WIDTH), lambda h, info: (0, heads + h))
     small = pl.BlockSpec((groups, 2, 8, WIDTH), lambda h, info: (0, h, 0, 0))
-    return pl.pallas_call(
-        attention_kernel,
+    shared = [] if x is None else [x]
+
+    def body(info, *refs):
+        attention_kernel(info, *refs[:6], *refs[6 + len(shared) :])
+
+    return pl.pallas_call(
+        body,
         grid_spec=pltpu.PrefetchScalarGridSpec(
             num_scalar_prefetch=1,
             grid=(heads,),
-            in_specs=[wide, wide, narrow, narrow, narrow, narrow],
-            out_specs=[pl.BlockSpec((groups, 2, 8, 3 * WIDTH), lambda h, info: (0, h, 0, 0)), small, small],
+            in_specs=[wide, wide, narrow, narrow, first_key, first_value]
+            + [pl.BlockSpec(memory_space=pl.ANY)] * len(shared),
+            out_specs=[pl.BlockSpec((groups, 2, 8, 3 * WIDTH), lambda h, info: (0, base + h, 0, 0)), small, small],
         ),
         out_shape=[
-            jax.ShapeDtypeStruct((groups, 2 * heads, 8, 3 * WIDTH), jnp.bfloat16),
+            jax.ShapeDtypeStruct((groups, 2 * all_heads, 8, 3 * WIDTH), jnp.bfloat16),
             jax.ShapeDtypeStruct((groups, 2 * heads, 8, WIDTH), jnp.float32),
             jax.ShapeDtypeStruct((groups, 2 * heads, 8, WIDTH), jnp.bfloat16),
         ],
-        compiler_params=pltpu.CompilerParams(vmem_limit_bytes=32 * 1024 * 1024),
-        name="attention",
-    )(info, q, g, k, v, kp, vp)
-
-
-def combine_kernel(own_ref, part_ref, x_in, x_ref):
-    del x_in
-    x_ref[...] = (own_ref[...] + part_ref[...].astype(jnp.float32)).astype(jnp.bfloat16)
-
-
-def combine(own, part, x):
-    whole = pl.BlockSpec(own.shape, lambda i: (0, 0, 0, 0))
+        input_output_aliases={7: 0} if shared else {},
+        compiler_params=pltpu.CompilerParams(vmem_limit_bytes=VMEM_ATT * 1024 * 1024),
+        name=f"attention{chunk}",
+    )(info, q, g, k, v, first, first, *shared)
+
+
+def combine_kernel(*refs):
+    chunks = (len(refs) - 2) // 2
+    x_ref = refs[-1]
+    for c in range(chunks):
+        own_ref, part_ref = refs[2 * c], refs[2 * c + 1]
+        size = own_ref.shape[1]
+        total = own_ref[...] + part_ref[...].astype(jnp.float32)
+        x_ref[:, c * size : (c + 1) * size] = total.astype(jnp.bfloat16)
+
+
+def combine(owns, parts, x):
+    shape = x.shape[:3] + (WIDTH,)
+    operands = [a for pair in zip(owns, parts) for a in pair]
     return pl.pallas_call(
         combine_kernel,
         grid=(1,),
-        in_specs=[whole, whole, pl.BlockSpec(memory_space=pl.ANY)],
-        out_specs=pl.BlockSpec(own.shape, lambda i: (0, 0, 0, 2)),
+        in_specs=[pl.BlockSpec(a.shape, lambda i: (0, 0, 0, 0)) for a in operands] + [pl.BlockSpec(memory_space=pl.ANY)],
+        out_specs=pl.BlockSpec(shape, lambda i: (0, 0, 0, 2)),
         out_shape=jax.ShapeDtypeStruct(x.shape, x.dtype),
-        input_output_aliases={2: 0},
-        compiler_params=pltpu.CompilerParams(vmem_limit_bytes=32 * 1024 * 1024),
+        input_output_aliases={len(operands): 0},
+        compiler_params=pltpu.CompilerParams(vmem_limit_bytes=16 * 1024 * 1024),
         name="combine",
-    )(own, part, x)
-
-
-def reorder_kernel(pack_of, pack_offset, y_ref, x_ref, sem):
-    pairs = y_ref.shape[0]
-
+    )(*operands, x)
+
+
+def reorder_kernel(pack_of, pack_offset, y_ref, x_ref):
     def step(i, carry):
         block = pack_of[i] * (1024 // PAIR) + pack_offset[i] // PAIR
-        pltpu.make_async_copy(y_ref.at[i], x_ref.at[block], sem).start()
+        x_ref[block] = y_ref[i]
         return carry
 
-    lax.fori_loop(0, pairs, step, 0)
-    pltpu.make_async_copy(y_ref, x_ref, sem).wait()
+    lax.fori_loop(0, y_ref.shape[0], step, 0, unroll=8)
 
 
 def reorder(pack_of, pack_offset, y):
+    whole = pl.BlockSpec(y.shape, lambda i, *_: (0,) * y.ndim)
     return pl.pallas_call(
         reorder_kernel,
         grid_spec=pltpu.PrefetchScalarGridSpec(
-            num_scalar_prefetch=2,
-            grid=(1,),
-            in_specs=[pl.BlockSpec(memory_space=pl.ANY)],
-            out_specs=pl.BlockSpec(memory_space=pl.ANY),
-            scratch_shapes=[pltpu.SemaphoreType.DMA],
+            num_scalar_prefetch=2, grid=(1,), in_specs=[whole], out_specs=whole
         ),
         out_shape=jax.ShapeDtypeStruct(y.shape, y.dtype),
+        compiler_params=pltpu.CompilerParams(vmem_limit_bytes=16 * 1024 * 1024),
         name="reorder",
     )(pack_of, pack_offset, y)
 
@@ -166,11 +180,15 @@
 
     up = [(i, i + 1) for i in range(0, tensor_count, 2)]
     down = [(i + 1, i) for i in range(0, tensor_count, 2)]
-    first_keys = lax.ppermute(keys, "tensor", up)
-    first_values = lax.ppermute(values, "tensor", up)
-    pieces, own, part = attention(info, queries, grad_out, keys, values, first_keys, first_values)
-    part = lax.ppermute(part, "tensor", down)
-    pieces = combine(own, part, pieces)
+    span = keys.shape[1] // CHUNKS
+    cuts = [slice(c * span, (c + 1) * span) for c in range(CHUNKS)]
+    firsts = [lax.ppermute(jnp.concatenate([keys[:, cut], values[:, cut]], axis=1), "tensor", up) for cut in cuts]
+    pieces, owns, parts = None, [], []
+    for c in range(CHUNKS):
+        pieces, own, part = attention(info, queries, grad_out, keys, values, firsts[c], c, CHUNKS, pieces)
+        owns.append(own)
+        parts.append(lax.ppermute(part, "tensor", down))
+    pieces = combine(owns, parts, pieces)
     shape = pieces.shape
     spread = lax.all_to_all(pieces.reshape(devices, 8, 3 * WIDTH), BOTH, split_axis=0, concat_axis=0, tiled=True)
     ordered = reorder(pack_of, pack_offset, spread.reshape(devices // 2, 2, 8, 3 * WIDTH))

time: 204 us -> 145 us (0.71)
  Pallas kernels: 61.2 us -> 13.7 us
  waiting for transfers between devices: 20.1 us -> 8.21 us
    pallas_call x1, Pallas kernels: 49.5 us -> 1.42 us  [reorder(): pl.pallas_call(reorder_kernel, grid_spec=pltpu.PrefetchScalarGridSpec(num...]
    ppermute x3 -> x4, waiting for transfers between devices: 20.1 us -> 8.21 us  [the longest x2 5.95 us: per_device(): parts.append(lax.ppermute(part, 'tensor', down))]
    unnamed x8 -> x14, local copies, waits for them, and re-layouts: 4.35 us -> 1.93 us
    ppermute x3 -> x4, starting transfers between devices: 6.99 us -> 8.28 us  [the longest x2 5.69 us: per_device(): lax.ppermute(jnp.concatenate([keys[:, cut], values[:, cut]], axis=1), 'te...]
    pallas_call x2 -> x3, Pallas kernels: 8.77 us -> 9.39 us  [the longest x2 9.12 us: attention(): pl.pallas_call(body, grid_spec=pltpu.PrefetchScalarGridSpec(num_scalar_pr...]
  transfers between devices with their start and end apart: 3 -> 4, of which waited for: 3 -> 3; matrix products, arithmetic and copies ran while one was open for 1% -> 1% of each run, Pallas kernels for 0% -> 6%
where the time goes in v2:
time: 145 us; the launch traced here: 144 us
  blocking collectives  109 us (75%)
  Pallas kernels  13.7 us (9%)
  starting transfers between devices  8.28 us (6%)
  waiting for transfers between devices  8.21 us (6%)
  local copies, waits for them, and re-layouts  3.79 us (3%)
    all_to_all x1, blocking collectives, per_device(): lax.all_to_all(pieces.reshape(devices, 8, 3 * WIDTH), BOTH, split_axis=0,...  59.8 us
    all_to_all x1, blocking collectives, per_device(): lax.all_to_all(ordered.reshape(devices, 8, 3 * WIDTH), BOTH, split_axis=0...  48.9 us
    pallas_call x2, Pallas kernels, attention(): pl.pallas_call(body, grid_spec=pltpu.PrefetchScalarGridSpec(num_scalar_pr...  9.12 us
    ppermute x2, waiting for transfers between devices, per_device(): parts.append(lax.ppermute(part, 'tensor', down))  5.95 us
    ppermute x2, starting transfers between devices, per_device(): lax.ppermute(jnp.concatenate([keys[:, cut], values[:, cut]], axis=1), 'te...  5.69 us
    pallas_call x1, Pallas kernels, place(): pl.pallas_call(place_kernel, grid=(heads,), in_specs=[pl.BlockSpec((group...  2.94 us
  transfers between devices with their start and end apart: 4, of which 3 were waited for; matrix products, arithmetic and copies ran while one was open for 1% of the time, Pallas kernels for 6%

profile of v2, /device:TPU:1, one launch (start us, length us, event | category | flops | bytes accessed | tf_op | source)
XLA Modules:
  0.0 144.3 jit_solution(5233105226134616456)
XLA Ops:
  0.6 0.0 copy-start.6
  0.6 0.0 copy-start.1
  0.7 0.0 copy-start
  0.7 1.3 fusion
  2.0 4.4 %collective-permute-start = (bf16[128,1024]{1,0:T(8,128)(2,1)S(1)}, bf16[128,1024]{1,0:T(8,128)(2,1)S(1)}, u32[]{:S(2)}, u32[]{:S(2)}) collective-permute-start(bf16[128,1024]{1,0:T(8,128)(2,1)S(1)} %pad_maximum_fusion), channel_id=1, source_target_pairs={{0,1},{2,3},{4,5},{6,7},{8,9},{10,11},{12,13},{14,15},{16,17},{18,... | collective-permute-start | bytes 786440 | tf_op jit(solution)/shard_map/ppermute | solution.py:185
  6.4 1.3 collective-permute-start.2
  7.7 0.0 copy-done.6
  7.7 0.6 dynamic_slice.3
  8.3 0.7 pad_add_fusion.info
  9.0 2.3 %collective-permute-done.refs_4_.refs_5_ = bf16[128,1024]{1,0:T(8,128)(2,1)S(1)} collective-permute-done((bf16[128,1024]{1,0:T(8,128)(2,1)S(1)}, bf16[128,1024]{1,0:T(8,128)(2,1)S(1)}, u32[]{:S(2)}, u32[]{:S(2)}) %collective-permute-start) | collective-permute-done | bytes 262176 | tf_op jit(solution)/shard_map/ppermute | solution.py:185
  11.3 0.0 copy-done.1
  11.3 0.0 copy-done
  11.3 0.0 copy-start.2
  11.3 0.9 copy-done.2
  12.3 0.0 copy-start.3
  12.3 0.9 copy-done.3
  13.2 4.6 %attention0.1 = (bf16[16,16,8,384]{3,2,1,0:T(8,128)(2,1)S(1)}, f32[16,8,8,128]{3,2,1,0:T(8,128)S(1)}, bf16[16,8,8,128]{3,2,1,0:T(8,128)(2,1)S(1)}) custom-call(s32[2]{0:T(128)S(1)} %pad_add_fusion.info, bf16[128,4096]{1,0:T(8,128)(2,1)S(1)} %copy-done, bf16[128,4096]{1,0:T(8,128)(2,1)S(1)} %copy-done.1, bf16[128,1024]{1,0:T(8,128)(2,1)S(1)} %copy-done.2, ...), custom_call_target="tpu_custom_call" | custom-call | tf_op jit(solution)/shard_map/attention0/pallas_call | solution.py:78
  17.8 1.3 collective-permute-start.1
  19.1 0.0 collective-permute-done.2.refs_4_.refs_5_
  19.1 4.6 %attention1.1 = (bf16[16,16,8,384]{3,2,1,0:T(8,128)(2,1)S(1)}, f32[16,8,8,128]{3,2,1,0:T(8,128)S(1)}, bf16[16,8,8,128]{3,2,1,0:T(8,128)(2,1)S(1)}) custom-call(s32[2]{0:T(128)S(1)} %pad_add_fusion.info, bf16[128,4096]{1,0:T(8,128)(2,1)S(1)} %copy-done, bf16[128,4096]{1,0:T(8,128)(2,1)S(1)} %copy-done.1, ...), custom_call_target="tpu_custom_call", output_to_operand_aliasing={{0}: (7, {})} | custom-call | tf_op jit(solution)/shard_map/attention1/pallas_call | solution.py:78
  23.7 1.3 collective-permute-start.3
  25.0 0.1 collective-permute-done.1.refs_1_
  25.0 5.9 %collective-permute-done.3.refs_3_ = bf16[16,8,8,128]{3,2,1,0:T(8,128)(2,1)S(1)} collective-permute-done((bf16[16,8,8,128]{3,2,1,0:T(8,128)(2,1)S(1)}, bf16[16,8,8,128]{3,2,1,0:T(8,128)(2,1)S(1)}, u32[]{:S(2)}, u32[]{:S(2)}) %collective-permute-start.3) | collective-permute-done | bytes 262176 | tf_op jit(solution)/shard_map/ppermute | solution.py:190
  30.9 0.3 combine.1
  31.2 0.0 copy-start.4
  31.2 0.0 copy-start.5
  31.2 59.8 %all_to_all.10 = bf16[256,8,384]{2,1,0:T(8,128)(2,1)S(1)} all-to-all(bf16[256,8,384]{2,1,0:T(8,128)(2,1)S(1)} %bitcast.5), channel_id=1, replica_groups=mesh['dp'=32,'tensor'=8] {'dp','tensor'}, dimensions={0} | all-to-all | bytes 3145728 | tf_op jit(solution)/shard_map/all_to_all | solution.py:193
  91.0 0.0 copy-done.4
  91.0 0.0 copy-done.5
  91.0 1.4 reorder.1
  92.4 48.9 %all_to_all.11 = bf16[256,8,384]{2,1,0:T(8,128)(2,1)S(1)} all-to-all(bf16[256,8,384]{2,1,0:T(8,128)(2,1)S(1)} %bitcast.8), channel_id=1, replica_groups=mesh['dp'=32,'tensor'=8] {'dp','tensor'}, dimensions={0} | all-to-all | bytes 3145728 | tf_op jit(solution)/shard_map/all_to_all | solution.py:195
  141.3 2.9 %place.1 = (bf16[128,4096]{1,0:T(8,128)(2,1)}, bf16[128,1024]{1,0:T(8,128)(2,1)}, bf16[128,1024]{1,0:T(8,128)(2,1)}) custom-call(bf16[16,16,8,384]{3,2,1,0:T(8,128)(2,1)S(1)} %bitcast.6), custom_call_target="tpu_custom_call" | custom-call | tf_op jit(solution)/shard_map/place/pallas_call | solution.py:159
  (2 shorter events, 0.0 us)
Async XLA Ops:
  0.6 7.1 %copy-start.6 = (s32[128]{0:T(128)S(1)}, s32[128]{0:T(128)}, u32[]{:S(2)}) copy-start(s32[128]{0:T(128)} %param.11) | copy-start | bytes 1540
  0.6 10.7 %copy-start.1 = (bf16[128,4096]{1,0:T(8,128)(2,1)S(1)}, bf16[128,4096]{1,0:T(8,128)(2,1)}, u32[]{:S(2)}) copy-start(bf16[128,4096]{1,0:T(8,128)(2,1)} %refs_1_.3) | copy-start | bytes 3145732
  0.7 10.7 %copy-start = (bf16[128,4096]{1,0:T(8,128)(2,1)S(1)}, bf16[128,4096]{1,0:T(8,128)(2,1)}, u32[]{:S(2)}) copy-start(bf16[128,4096]{1,0:T(8,128)(2,1)} %refs_0_.3) | copy-start | bytes 3145732
  2.0 9.3 %collective-permute-start = (bf16[128,1024]{1,0:T(8,128)(2,1)S(1)}, bf16[128,1024]{1,0:T(8,128)(2,1)S(1)}, u32[]{:S(2)}, u32[]{:S(2)}) collective-permute-start(bf16[128,1024]{1,0:T(8,128)(2,1)S(1)} %pad_maximum_fusion), channel_id=1, source_target_pairs={{0,1},{2,3},{4,5},{6,7},{8,9},{10,11},{12,13},{14,15},{16,17},{18,... | collective-permute-start | bytes 786440 | tf_op jit(solution)/shard_map/ppermute | solution.py:185
  6.4 12.7 %collective-permute-start.2 = (bf16[128,1024]{1,0:T(8,128)(2,1)S(1)}, bf16[128,1024]{1,0:T(8,128)(2,1)S(1)}, u32[]{:S(2)}, u32[]{:S(2)}) collective-permute-start(bf16[128,1024]{1,0:T(8,128)(2,1)S(1)} %pad_maximum_fusion.1), channel_id=1, source_target_pairs={{0,1},{2,3},{4,5},{6,7},{8,9},{10,11},{12,13},{14,15},{16,17},{18,... | collective-permute-start | bytes 786440 | tf_op jit(solution)/shard_map/ppermute | solution.py:185
  11.3 1.0 copy-start.2
  12.3 0.9 copy-start.3
  17.8 7.2 %collective-permute-start.1 = (bf16[16,8,8,128]{3,2,1,0:T(8,128)(2,1)S(1)}, bf16[16,8,8,128]{3,2,1,0:T(8,128)(2,1)S(1)}, u32[]{:S(2)}, u32[]{:S(2)}) collective-permute-start(bf16[16,8,8,128]{3,2,1,0:T(8,128)(2,1)S(1)} %get-tuple-element.10), channel_id=1, source_target_pairs={{1,0},{3,2},{5,4},{7,6},{9,8},{11,10},{13,12},{15,14},{17,16},{19,... | collective-permute-start | bytes 786440 | tf_op jit(solution)/shard_map/ppermute | solution.py:190
  23.7 7.3 %collective-permute-start.3 = (bf16[16,8,8,128]{3,2,1,0:T(8,128)(2,1)S(1)}, bf16[16,8,8,128]{3,2,1,0:T(8,128)(2,1)S(1)}, u32[]{:S(2)}, u32[]{:S(2)}) collective-permute-start(bf16[16,8,8,128]{3,2,1,0:T(8,128)(2,1)S(1)} %get-tuple-element.13), channel_id=1, source_target_pairs={{1,0},{3,2},{5,4},{7,6},{9,8},{11,10},{13,12},{15,14},{17,16},{19,... | collective-permute-start | bytes 786440 | tf_op jit(solution)/shard_map/ppermute | solution.py:190
  31.2 59.8 %copy-start.4 = (s32[128]{0:T(128)S(1)}, s32[128]{0:T(128)}, u32[]{:S(2)}) copy-start(s32[128]{0:T(128)} %pack_of.1) | copy-start | bytes 1540
  31.2 59.8 %copy-start.5 = (s32[128]{0:T(128)S(1)}, s32[128]{0:T(128)}, u32[]{:S(2)}) copy-start(s32[128]{0:T(128)} %pack_offset.1) | copy-start | bytes 1540

commit v3 on v2

v3 whole, which is shorter than its diff:
```python
import functools
import math

import jax
import jax.numpy as jnp
from jax import lax
from jax.experimental import pallas as pl
from jax.experimental.pallas import tpu as pltpu
from jax.sharding import PartitionSpec as P

WIDTH = 128
PAIR = 256
HALF = 128
GROUP = 4
CHUNKS = (4, 4)
VMEM_ATT = 32
PLACE_STEPS = 2
BOTH = ("dp", "tensor")
CONTRACT_LAST = (((1,), (1,)), ((), ()))
CONTRACT_FIRST = (((0,), (0,)), ((), ()))


def attention_kernel(lo, hi, info, q_ref, g_ref, own_ref, first_ref, dq_ref, mine_ref, part_ref):
    chosen = info[0]
    second = info[1]
    scale = 1.0 / math.sqrt(WIDTH)
    f32 = jnp.float32
    bf16 = jnp.bfloat16
    heads = hi - lo

    row = lax.broadcasted_iota(jnp.int32, (HALF, PAIR), 0) + HALF * second
    col = lax.broadcasted_iota(jnp.int32, (HALF, PAIR), 1) - HALF * (1 - second)
    low = jnp.where(row >= chosen, chosen, 0)
    allowed = (col >= low) & (col <= row)

    def four(ref, h):
        left = (lo + h) * GROUP * WIDTH
        return jnp.concatenate([ref[:, left + i * WIDTH : left + (i + 1) * WIDTH] for i in range(GROUP)], axis=0)

    def both(h):
        at = slice(h * WIDTH, (h + 1) * WIDTH)
        return jnp.concatenate([first_ref[:, at], own_ref[:, at]], axis=0)

    def tiles(block):
        return block.reshape(HALF // 8, 8, WIDTH)

    products = []
    for h in range(heads):
        scores = lax.dot_general(four(q_ref, h), both(h), CONTRACT_LAST, preferred_element_type=f32)
        dprob = lax.dot_general(four(g_ref, h), both(heads + h), CONTRACT_LAST, preferred_element_type=f32)
        products.append((scores, dprob))
    factors = []
    for scores, dprob in products:
        scores = jnp.where(allowed[None], scores.reshape(GROUP, HALF, PAIR), -1e30).reshape(GROUP * HALF, PAIR)
        peak = jnp.max(scores, axis=1, keepdims=True)
        weights = jnp.exp2((scores - peak) * (scale * math.log2(math.e)))
        probs = weights * (1.0 / jnp.sum(weights, axis=1, keepdims=True))
        probs_b = probs.astype(bf16)
        delta = jnp.sum(probs_b.astype(f32) * dprob, axis=1, keepdims=True)
        factors.append((probs_b, (probs * (dprob - delta)).astype(bf16)))
    for h, (probs_b, dscore_b) in enumerate(factors):
        dq = jnp.dot(dscore_b, both(h), preferred_element_type=f32) * scale
        dk = lax.dot_general(dscore_b, four(q_ref, h), CONTRACT_FIRST, preferred_element_type=f32) * scale
        dv = lax.dot_general(probs_b, four(g_ref, h), CONTRACT_FIRST, preferred_element_type=f32)
        for i in range(GROUP):
            at = slice((i % 2) * WIDTH, (i % 2 + 1) * WIDTH)
            dq_ref[:, 2 * h + i // 2, :, at] = tiles(dq[i * HALF : (i + 1) * HALF]).astype(bf16)
        mine_ref[:, 2 * h] = tiles(dk[HALF:])
        mine_ref[:, 2 * h + 1] = tiles(dv[HALF:])
        part_ref[:, 2 * h] = tiles(dk[:HALF]).astype(bf16)
        part_ref[:, 2 * h + 1] = tiles(dv[:HALF]).astype(bf16)


def whole(shape):
    return pl.BlockSpec(shape, lambda i, *_: (0,) * len(shape))


def attention(info, q, g, own, first, lo, hi):
    rows = (HALF // 8, 2 * (hi - lo), 8)
    outs = [
        jax.ShapeDtypeStruct(rows + (2 * WIDTH,), jnp.bfloat16),
        jax.ShapeDtypeStruct(rows + (WIDTH,), jnp.float32),
        jax.ShapeDtypeStruct(rows + (WIDTH,), jnp.bfloat16),
    ]
    return pl.pallas_call(
        functools.partial(attention_kernel, lo, hi),
        grid_spec=pltpu.PrefetchScalarGridSpec(
            num_scalar_prefetch=1,
            grid=(1,),
            in_specs=[whole(a.shape) for a in (q, g, own, first)],
            out_specs=[whole(a.shape) for a in outs],
        ),
        out_shape=outs,
        compiler_params=pltpu.CompilerParams(vmem_limit_bytes=VMEM_ATT * 1024 * 1024),
        name=f"attention{lo}",
    )(info, q, g, own, first)


def combine_kernel(*refs):
    x_ref = refs[-1]
    at = 0
    for c in range(len(refs) // 3):
        dq_ref, mine_ref, part_ref = refs[3 * c : 3 * c + 3]
        size = dq_ref.shape[1]
        total = mine_ref[...] + part_ref[...].astype(jnp.float32)
        x_ref[:, at : at + size, :, : 2 * WIDTH] = dq_ref[...]
        x_ref[:, at : at + size, :, 2 * WIDTH :] = total.astype(jnp.bfloat16)
        at += size


def combine(parts, heads):
    shape = (HALF // 8, 2 * heads, 8, 3 * WIDTH)
    operands = [a for part in parts for a in part]
    return pl.pallas_call(
        combine_kernel,
        grid=(1,),
        in_specs=[whole(a.shape) for a in operands],
        out_specs=whole(shape),
        out_shape=jax.ShapeDtypeStruct(shape, jnp.bfloat16),
        compiler_params=pltpu.CompilerParams(vmem_limit_bytes=16 * 1024 * 1024),
        name="combine",
    )(*operands)


def reorder_kernel(pack_of, pack_offset, y_ref, x_ref):
    def step(i, carry):
        block = pack_of[i] * (1024 // PAIR) + pack_offset[i] // PAIR
        x_ref[block] = y_ref[i]
        return carry

    lax.fori_loop(0, y_ref.shape[0], step, 0, unroll=8)


def reorder(pack_of, pack_offset, y):
    return pl.pallas_call(
        reorder_kernel,
        grid_spec=pltpu.PrefetchScalarGridSpec(
            num_scalar_prefetch=2, grid=(1,), in_specs=[whole(y.shape)], out_specs=whole(y.shape)
        ),
        out_shape=jax.ShapeDtypeStruct(y.shape, y.dtype),
        compiler_params=pltpu.CompilerParams(vmem_limit_bytes=16 * 1024 * 1024),
        name="reorder",
    )(pack_of, pack_offset, y)


def place_kernel(z_ref, q_ref, k_ref, v_ref):
    def rows(block):
        return block.astype(jnp.float32).reshape(HALF, block.shape[-1]).astype(jnp.bfloat16)

    for h in range(z_ref.shape[1] // 2):
        left = h * GROUP * WIDTH
        q_ref[:, left : left + 2 * WIDTH] = rows(z_ref[:, 2 * h, :, : 2 * WIDTH])
        q_ref[:, left + 2 * WIDTH : left + 4 * WIDTH] = rows(z_ref[:, 2 * h + 1, :, : 2 * WIDTH])
        k_ref[:, h * WIDTH : (h + 1) * WIDTH] = rows(z_ref[:, 2 * h, :, 2 * WIDTH :])
        v_ref[:, h * WIDTH : (h + 1) * WIDTH] = rows(z_ref[:, 2 * h + 1, :, 2 * WIDTH :])


def place(z):
    groups, double, _, _ = z.shape
    heads = double // 2
    step = heads // PLACE_STEPS
    narrow = pl.BlockSpec((HALF, step * WIDTH), lambda h: (0, h))
    return pl.pallas_call(
        place_kernel,
        grid=(PLACE_STEPS,),
        in_specs=[pl.BlockSpec((groups, 2 * step, 8, 3 * WIDTH), lambda h: (0, h, 0, 0))],
        out_specs=[pl.BlockSpec((HALF, step * GROUP * WIDTH), lambda h: (0, h)), narrow, narrow],
        out_shape=[
            jax.ShapeDtypeStruct((HALF, heads * GROUP * WIDTH), jnp.bfloat16),
            jax.ShapeDtypeStruct((HALF, heads * WIDTH), jnp.bfloat16),
            jax.ShapeDtypeStruct((HALF, heads * WIDTH), jnp.bfloat16),
        ],
        compiler_params=pltpu.CompilerParams(vmem_limit_bytes=32 * 1024 * 1024),
        name="place",
    )(z)


def per_device(queries, keys, values, grad_out, chosen_len, pack_of, pack_offset):
    tensor_count = lax.axis_size("tensor")
    devices = tensor_count * lax.axis_size("dp")
    tensor_here = lax.axis_index("tensor")
    device_here = lax.axis_index("dp") * tensor_count + tensor_here
    info = jnp.stack([chosen_len[device_here // 2], tensor_here % 2]).astype(jnp.int32)

    up = [(i, i + 1) for i in range(0, tensor_count, 2)]
    down = [(i + 1, i) for i in range(0, tensor_count, 2)]
    heads = keys.shape[1] // WIDTH
    bounds = [0]
    for share in CHUNKS:
        bounds.append(bounds[-1] + share * heads // sum(CHUNKS))
    cuts = list(zip(bounds[:-1], bounds[1:]))
    owns = [
        jnp.concatenate([keys[:, lo * WIDTH : hi * WIDTH], values[:, lo * WIDTH : hi * WIDTH]], axis=1)
        for lo, hi in cuts
    ]
    firsts = [lax.ppermute(own, "tensor", up) for own in owns]
    parts = []
    for (lo, hi), own, first in zip(cuts, owns, firsts):
        dq, mine, part = attention(info, queries, grad_out, own, first, lo, hi)
        parts.append((dq, mine, lax.ppermute(part, "tensor", down)))
    pieces = combine(parts, heads)
    shape = pieces.shape
    spread = lax.all_to_all(pieces.reshape(devices, 8, 3 * WIDTH), BOTH, split_axis=0, concat_axis=0, tiled=True)
    ordered = reorder(pack_of, pack_offset, spread.reshape(devices // 2, 2, 8, 3 * WIDTH))
    gathered = lax.all_to_all(ordered.reshape(devices, 8, 3 * WIDTH), BOTH, split_axis=0, concat_axis=0, tiled=True)
    return tuple(place(gathered.reshape(shape)))


def solution(mesh):
    rows = P(BOTH, None)
    return jax.shard_map(
        per_device,
        mesh=mesh,
        in_specs=(rows, rows, rows, rows, P(), P(), P()),
        out_specs=(rows, rows, rows),
        check_vma=False,
    )
```

time: 145 us -> 139 us (0.959)
  Pallas kernels: 13.7 us -> 9.12 us
  waiting for transfers between devices: 8.21 us -> 11.1 us
  blocking collectives: 109 us -> 107 us
  local copies, waits for them, and re-layouts: 3.79 us -> 1.89 us
    pallas_call x4, Pallas kernels: 12.3 us -> 7.7 us  [the longest x2 6.12 us: attention(): pl.pallas_call(functools.partial(attention_kernel, lo, hi), grid_spec=plt...]
    ppermute x4, waiting for transfers between devices: 8.21 us -> 11.1 us  [the longest x2 7.54 us: per_device(): parts.append((dq, mine, lax.ppermute(part, 'tensor', down)))]
    unnamed x14 -> x10, local copies, waits for them, and re-layouts: 1.93 us -> 0.03 us
    all_to_all x1, blocking collectives: 59.8 us -> 58.2 us  [per_device(): lax.all_to_all(pieces.reshape(devices, 8, 3 * WIDTH), BOTH, split_axis=0,...]
  transfers between devices with their start and end apart: 4 -> 4, of which waited for: 3 -> 4; matrix products, arithmetic and copies ran while one was open for 1% -> 1% of each run, Pallas kernels for 6% -> 4%
where the time goes in v3:
time: 139 us
  blocking collectives  107 us (77%)
  waiting for transfers between devices  11.1 us (8%)
  Pallas kernels  9.12 us (7%)
  starting transfers between devices  8.28 us (6%)
  local copies, waits for them, and re-layouts  1.89 us (1%)
    all_to_all x1, blocking collectives, per_device(): lax.all_to_all(pieces.reshape(devices, 8, 3 * WIDTH), BOTH, split_axis=0,...  58.2 us
    all_to_all x1, blocking collectives, per_device(): lax.all_to_all(ordered.reshape(devices, 8, 3 * WIDTH), BOTH, split_axis=0...  48.9 us
    ppermute x2, waiting for transfers between devices, per_device(): parts.append((dq, mine, lax.ppermute(part, 'tensor', down)))  7.54 us
    pallas_call x2, Pallas kernels, attention(): pl.pallas_call(functools.partial(attention_kernel, lo, hi), grid_spec=plt...  6.12 us
    ppermute x2, starting transfers between devices, per_device(): firsts = [lax.ppermute(own, 'tensor', up) for own in owns]  5.69 us
    ppermute x2, waiting for transfers between devices, per_device(): firsts = [lax.ppermute(own, 'tensor', up) for own in owns]  3.51 us
  transfers between devices with their start and end apart: 4, of which 4 were waited for; matrix products, arithmetic and copies ran while one was open for 1% of the time, Pallas kernels for 4%

profile of v3, /device:TPU:1, one launch (start us, length us, event | category | flops | bytes accessed | tf_op | source)
XLA Modules:
  0.0 139.0 jit_solution(1170873724647473574)
XLA Ops:
  0.6 0.0 copy-start.4
  0.6 0.0 copy-start.1
  0.7 0.0 copy-start
  0.7 1.3 fusion
  2.0 4.4 %collective-permute-start.2 = (bf16[128,1024]{1,0:T(8,128)(2,1)S(1)}, bf16[128,1024]{1,0:T(8,128)(2,1)S(1)}, u32[]{:S(2)}, u32[]{:S(2)}) collective-permute-start(bf16[128,1024]{1,0:T(8,128)(2,1)S(1)} %pad_maximum_fusion.1.own_ref), channel_id=1, source_target_pairs={{0,1},{2,3},{4,5},{6,7},{8,9},{10,11},{12,13},{14,15},{16,17},{18,... | collective-permute-start | bytes 786440 | tf_op jit(solution)/shard_map/ppermute | solution.py:196
  6.4 1.3 collective-permute-start
  7.7 0.0 copy-done.4
  7.7 0.6 dynamic_slice.3
  8.3 0.7 pad_add_fusion.info
  9.0 2.3 %collective-permute-done.2.first_ref = bf16[128,1024]{1,0:T(8,128)(2,1)S(1)} collective-permute-done((bf16[128,1024]{1,0:T(8,128)(2,1)S(1)}, bf16[128,1024]{1,0:T(8,128)(2,1)S(1)}, u32[]{:S(2)}, u32[]{:S(2)}) %collective-permute-start.2) | collective-permute-done | bytes 262176 | tf_op jit(solution)/shard_map/ppermute | solution.py:196
  11.3 0.0 copy-done.1
  11.3 0.0 copy-done
  11.3 3.1 %attention4.1 = (bf16[16,8,8,256]{3,2,1,0:T(8,128)(2,1)S(1)}, f32[16,8,8,128]{3,2,1,0:T(8,128)S(1)}, bf16[16,8,8,128]{3,2,1,0:T(8,128)(2,1)S(1)}) custom-call(s32[2]{0:T(128)S(1)} %pad_add_fusion.info, bf16[128,4096]{1,0:T(8,128)(2,1)S(1)} %copy-done, bf16[128,4096]{1,0:T(8,128)(2,1)S(1)} %copy-done.1, bf16[128,1024]{1,0:T(8,128)(2,1)S(1)} %pad_maximum_fusion.1.own_ref, ...), custom_call_target="tpu_custom_call" | custom-call | tf_op jit(solution)/shard_map/attention4/pallas_call | solution.py:85
  14.4 1.3 collective-permute-start.3
  15.7 1.2 collective-permute-done.first_ref
  16.9 3.1 %attention0.1 = (bf16[16,8,8,256]{3,2,1,0:T(8,128)(2,1)S(1)}, f32[16,8,8,128]{3,2,1,0:T(8,128)S(1)}, bf16[16,8,8,128]{3,2,1,0:T(8,128)(2,1)S(1)}) custom-call(s32[2]{0:T(128)S(1)} %pad_add_fusion.info, bf16[128,4096]{1,0:T(8,128)(2,1)S(1)} %copy-done, bf16[128,4096]{1,0:T(8,128)(2,1)S(1)} %copy-done.1, bf16[128,1024]{1,0:T(8,128)(2,1)S(1)} %pad_maximum_fusion.own_ref, ...), custom_call_target="tpu_custom_call" | custom-call | tf_op jit(solution)/shard_map/attention0/pallas_call | solution.py:85
  20.0 1.3 collective-permute-start.1
  21.3 0.3 collective-permute-done.3.refs_5_
  21.6 7.2 %collective-permute-done.1.refs_2_ = bf16[16,8,8,128]{3,2,1,0:T(8,128)(2,1)S(1)} collective-permute-done((bf16[16,8,8,128]{3,2,1,0:T(8,128)(2,1)S(1)}, bf16[16,8,8,128]{3,2,1,0:T(8,128)(2,1)S(1)}, u32[]{:S(2)}, u32[]{:S(2)}) %collective-permute-start.1) | collective-permute-done | bytes 262176 | tf_op jit(solution)/shard_map/ppermute | solution.py:200
  28.8 0.2 combine.1
  29.0 0.0 copy-start.2
  29.0 0.0 copy-start.3
  29.0 58.2 %all_to_all.10 = bf16[256,8,384]{2,1,0:T(8,128)(2,1)S(1)} all-to-all(bf16[256,8,384]{2,1,0:T(8,128)(2,1)S(1)} %bitcast.8), channel_id=1, replica_groups=mesh['dp'=32,'tensor'=8] {'dp','tensor'}, dimensions={0} | all-to-all | bytes 3145728 | tf_op jit(solution)/shard_map/all_to_all | solution.py:203
  87.2 0.0 copy-done.2
  87.2 0.0 copy-done.3
  87.3 1.4 %reorder.1 = bf16[128,2,8,384]{3,2,1,0:T(8,128)(2,1)S(1)} custom-call(s32[128]{0:T(128)S(1)} %copy-done.2, s32[128]{0:T(128)S(1)} %copy-done.3, bf16[128,2,8,384]{3,2,1,0:T(8,128)(2,1)S(1)} %bitcast.6), custom_call_target="tpu_custom_call" | custom-call | tf_op jit(solution)/shard_map/reorder/pallas_call | solution.py:135
  88.7 48.9 %all_to_all.11 = bf16[256,8,384]{2,1,0:T(8,128)(2,1)S(1)} all-to-all(bf16[256,8,384]{2,1,0:T(8,128)(2,1)S(1)} %bitcast.7), channel_id=1, replica_groups=mesh['dp'=32,'tensor'=8] {'dp','tensor'}, dimensions={0} | all-to-all | bytes 3145728 | tf_op jit(solution)/shard_map/all_to_all | solution.py:205
  137.6 1.4 %place.1 = (bf16[128,4096]{1,0:T(8,128)(2,1)}, bf16[128,1024]{1,0:T(8,128)(2,1)}, bf16[128,1024]{1,0:T(8,128)(2,1)}) custom-call(bf16[16,16,8,384]{3,2,1,0:T(8,128)(2,1)S(1)} %bitcast.5), custom_call_target="tpu_custom_call" | custom-call | tf_op jit(solution)/shard_map/place/pallas_call | solution.py:163
  (2 shorter events, 0.0 us)
Async XLA Ops:
  0.6 7.1 %copy-start.4 = (s32[128]{0:T(128)S(1)}, s32[128]{0:T(128)}, u32[]{:S(2)}) copy-start(s32[128]{0:T(128)} %param.11) | copy-start | bytes 1540
  0.6 10.7 %copy-start.1 = (bf16[128,4096]{1,0:T(8,128)(2,1)S(1)}, bf16[128,4096]{1,0:T(8,128)(2,1)}, u32[]{:S(2)}) copy-start(bf16[128,4096]{1,0:T(8,128)(2,1)} %g_ref.3) | copy-start | bytes 3145732
  0.7 10.7 %copy-start = (bf16[128,4096]{1,0:T(8,128)(2,1)S(1)}, bf16[128,4096]{1,0:T(8,128)(2,1)}, u32[]{:S(2)}) copy-start(bf16[128,4096]{1,0:T(8,128)(2,1)} %q_ref.3) | copy-start | bytes 3145732
  2.0 9.3 %collective-permute-start.2 = (bf16[128,1024]{1,0:T(8,128)(2,1)S(1)}, bf16[128,1024]{1,0:T(8,128)(2,1)S(1)}, u32[]{:S(2)}, u32[]{:S(2)}) collective-permute-start(bf16[128,1024]{1,0:T(8,128)(2,1)S(1)} %pad_maximum_fusion.1.own_ref), channel_id=1, source_target_pairs={{0,1},{2,3},{4,5},{6,7},{8,9},{10,11},{12,13},{14,15},{16,17},{18,... | collective-permute-start | bytes 786440 | tf_op jit(solution)/shard_map/ppermute | solution.py:196
  6.4 10.5 %collective-permute-start = (bf16[128,1024]{1,0:T(8,128)(2,1)S(1)}, bf16[128,1024]{1,0:T(8,128)(2,1)S(1)}, u32[]{:S(2)}, u32[]{:S(2)}) collective-permute-start(bf16[128,1024]{1,0:T(8,128)(2,1)S(1)} %pad_maximum_fusion.own_ref), channel_id=1, source_target_pairs={{0,1},{2,3},{4,5},{6,7},{8,9},{10,11},{12,13},{14,15},{16,17},{18,... | collective-permute-start | bytes 786440 | tf_op jit(solution)/shard_map/ppermute | solution.py:196
  14.4 7.2 %collective-permute-start.3 = (bf16[16,8,8,128]{3,2,1,0:T(8,128)(2,1)S(1)}, bf16[16,8,8,128]{3,2,1,0:T(8,128)(2,1)S(1)}, u32[]{:S(2)}, u32[]{:S(2)}) collective-permute-start(bf16[16,8,8,128]{3,2,1,0:T(8,128)(2,1)S(1)} %get-tuple-element.14), channel_id=1, source_target_pairs={{1,0},{3,2},{5,4},{7,6},{9,8},{11,10},{13,12},{15,14},{17,16},{19,... | collective-permute-start | bytes 786440 | tf_op jit(solution)/shard_map/ppermute | solution.py:200
  20.0 8.8 %collective-permute-start.1 = (bf16[16,8,8,128]{3,2,1,0:T(8,128)(2,1)S(1)}, bf16[16,8,8,128]{3,2,1,0:T(8,128)(2,1)S(1)}, u32[]{:S(2)}, u32[]{:S(2)}) collective-permute-start(bf16[16,8,8,128]{3,2,1,0:T(8,128)(2,1)S(1)} %get-tuple-element.11), channel_id=1, source_target_pairs={{1,0},{3,2},{5,4},{7,6},{9,8},{11,10},{13,12},{15,14},{17,16},{19,... | collective-permute-start | bytes 786440 | tf_op jit(solution)/shard_map/ppermute | solution.py:200
  29.0 58.2 %copy-start.2 = (s32[128]{0:T(128)S(1)}, s32[128]{0:T(128)}, u32[]{:S(2)}) copy-start(s32[128]{0:T(128)} %pack_of.1) | copy-start | bytes 1540
  29.0 58.2 %copy-start.3 = (s32[128]{0:T(128)S(1)}, s32[128]{0:T(128)}, u32[]{:S(2)}) copy-start(s32[128]{0:T(128)} %pack_offset.1) | copy-start | bytes 1540

commit v4 on v3

--- a/solution.py
+++ b/solution.py
@@ -15,14 +15,16 @@
 CHUNKS = (4, 4)
 VMEM_ATT = 32
 PLACE_STEPS = 2
-BOTH = ("dp", "tensor")
+TILE = 16
+PAIRS_OVER = ("dp", "slot")
+ALL = ("dp", "slot", "half")
 CONTRACT_LAST = (((1,), (1,)), ((), ()))
 CONTRACT_FIRST = (((0,), (0,)), ((), ()))
 
 
-def attention_kernel(lo, hi, info, q_ref, g_ref, own_ref, first_ref, dq_ref, mine_ref, part_ref):
-    chosen = info[0]
-    second = info[1]
+def attention_kernel(lo, hi, info_ref, q_ref, g_ref, own_ref, first_ref, dq_ref, mine_ref, part_ref):
+    chosen = info_ref[0:1, :]
+    second = info_ref[8:9, :]
     scale = 1.0 / math.sqrt(WIDTH)
     f32 = jnp.float32
     bf16 = jnp.bfloat16
@@ -42,7 +44,7 @@
         return jnp.concatenate([first_ref[:, at], own_ref[:, at]], axis=0)
 
     def tiles(block):
-        return block.reshape(HALF // 8, 8, WIDTH)
+        return block.reshape(HALF // TILE, TILE, WIDTH)
 
     products = []
     for h in range(heads):
@@ -75,25 +77,25 @@
     return pl.BlockSpec(shape, lambda i, *_: (0,) * len(shape))
 
 
-def attention(info, q, g, own, first, lo, hi):
-    rows = (HALF // 8, 2 * (hi - lo), 8)
+def attention(info, q, g, own, first, lo, hi, before):
+    rows = (HALF // TILE, 2 * (hi - lo), TILE)
     outs = [
         jax.ShapeDtypeStruct(rows + (2 * WIDTH,), jnp.bfloat16),
         jax.ShapeDtypeStruct(rows + (WIDTH,), jnp.float32),
         jax.ShapeDtypeStruct(rows + (WIDTH,), jnp.bfloat16),
     ]
-    return pl.pallas_call(
-        functools.partial(attention_kernel, lo, hi),
-        grid_spec=pltpu.PrefetchScalarGridSpec(
-            num_scalar_prefetch=1,
-            grid=(1,),
-            in_specs=[whole(a.shape) for a in (q, g, own, first)],
-            out_specs=[whole(a.shape) for a in outs],
-        ),
+    def body(*refs):
+        attention_kernel(lo, hi, *refs[:5], *refs[5 + len(before) :])
+
+    return pl.pallas_call(
+        body,
+        grid=(1,),
+        in_specs=[whole(a.shape) for a in (info, q, g, own, first)] + [pl.BlockSpec(memory_space=pl.ANY)] * len(before),
+        out_specs=[whole(a.shape) for a in outs],
         out_shape=outs,
         compiler_params=pltpu.CompilerParams(vmem_limit_bytes=VMEM_ATT * 1024 * 1024),
         name=f"attention{lo}",
-    )(info, q, g, own, first)
+    )(info, q, g, own, first, *before)
 
 
 def combine_kernel(*refs):
@@ -109,7 +111,7 @@
 
 
 def combine(parts, heads):
-    shape = (HALF // 8, 2 * heads, 8, 3 * WIDTH)
+    shape = (HALF // TILE, 2 * heads, TILE, 3 * WIDTH)
     operands = [a for part in parts for a in part]
     return pl.pallas_call(
         combine_kernel,
@@ -128,7 +130,7 @@
         x_ref[block] = y_ref[i]
         return carry
 
-    lax.fori_loop(0, y_ref.shape[0], step, 0, unroll=8)
+    lax.fori_loop(0, y_ref.shape[0], step, 0, unroll=32)
 
 
 def reorder(pack_of, pack_offset, y):
@@ -163,7 +165,7 @@
     return pl.pallas_call(
         place_kernel,
         grid=(PLACE_STEPS,),
-        in_specs=[pl.BlockSpec((groups, 2 * step, 8, 3 * WIDTH), lambda h: (0, h, 0, 0))],
+        in_specs=[pl.BlockSpec((groups, 2 * step, TILE, 3 * WIDTH), lambda h: (0, h, 0, 0))],
         out_specs=[pl.BlockSpec((HALF, step * GROUP * WIDTH), lambda h: (0, h)), narrow, narrow],
         out_shape=[
             jax.ShapeDtypeStruct((HALF, heads * GROUP * WIDTH), jnp.bfloat16),
@@ -176,14 +178,13 @@
 
 
 def per_device(queries, keys, values, grad_out, chosen_len, pack_of, pack_offset):
-    tensor_count = lax.axis_size("tensor")
-    devices = tensor_count * lax.axis_size("dp")
-    tensor_here = lax.axis_index("tensor")
-    device_here = lax.axis_index("dp") * tensor_count + tensor_here
-    info = jnp.stack([chosen_len[device_here // 2], tensor_here % 2]).astype(jnp.int32)
-
-    up = [(i, i + 1) for i in range(0, tensor_count, 2)]
-    down = [(i + 1, i) for i in range(0, tensor_count, 2)]
+    pairs = lax.axis_size("dp") * lax.axis_size("slot")
+    pair_here = lax.axis_index("dp") * lax.axis_size("slot") + lax.axis_index("slot")
+    half_here = lax.axis_index("half").reshape(1)
+    chosen_here = lax.dynamic_slice(chosen_len, (pair_here,), (1,))
+    info = jnp.where(jnp.arange(16)[:, None] < 8, chosen_here[None], half_here[None])
+    info = jnp.broadcast_to(info, (16, PAIR))
+
     heads = keys.shape[1] // WIDTH
     bounds = [0]
     for share in CHUNKS:
@@ -193,21 +194,25 @@
         jnp.concatenate([keys[:, lo * WIDTH : hi * WIDTH], values[:, lo * WIDTH : hi * WIDTH]], axis=1)
         for lo, hi in cuts
     ]
-    firsts = [lax.ppermute(own, "tensor", up) for own in owns]
+    firsts = [lax.ppermute(own, "half", [(0, 1)]) for own in owns]
     parts = []
     for (lo, hi), own, first in zip(cuts, owns, firsts):
-        dq, mine, part = attention(info, queries, grad_out, own, first, lo, hi)
-        parts.append((dq, mine, lax.ppermute(part, "tensor", down)))
+        before = [parts[-1][0]] if parts else []
+        dq, mine, part = attention(info, queries, grad_out, own, first, lo, hi, before)
+        parts.append((dq, mine, lax.ppermute(part, "half", [(1, 0)])))
     pieces = combine(parts, heads)
     shape = pieces.shape
-    spread = lax.all_to_all(pieces.reshape(devices, 8, 3 * WIDTH), BOTH, split_axis=0, concat_axis=0, tiled=True)
-    ordered = reorder(pack_of, pack_offset, spread.reshape(devices // 2, 2, 8, 3 * WIDTH))
-    gathered = lax.all_to_all(ordered.reshape(devices, 8, 3 * WIDTH), BOTH, split_axis=0, concat_axis=0, tiled=True)
+    piece = (pairs,) + shape[2:]
+    spread = lax.all_to_all(pieces.reshape(piece), PAIRS_OVER, split_axis=0, concat_axis=0, tiled=True)
+    ordered = reorder(pack_of, pack_offset, spread)
+    gathered = lax.all_to_all(ordered, PAIRS_OVER, split_axis=0, concat_axis=0, tiled=True)
     return tuple(place(gathered.reshape(shape)))
 
 
 def solution(mesh):
-    rows = P(BOTH, None)
+    shards, holders = mesh.devices.shape
+    mesh = jax.sharding.Mesh(mesh.devices.reshape(shards, holders // 2, 2), ALL)
+    rows = P(ALL, None)
     return jax.shard_map(
         per_device,
         mesh=mesh,

time: 139 us -> 138 us (level)
  no operation moved by 1% of the time
where the time goes in v4:
time: 138 us
  blocking collectives  106 us (77%)
  waiting for transfers between devices  11.7 us (8%)
  starting transfers between devices  8.28 us (6%)
  Pallas kernels  7.95 us (6%)
  local copies, waits for them, and re-layouts  1.96 us (1%)
    all_to_all x1, blocking collectives, per_device(): lax.all_to_all(pieces.reshape(piece), PAIRS_OVER, split_axis=0, concat_ax...  58.3 us
    all_to_all x1, blocking collectives, per_device(): lax.all_to_all(ordered, PAIRS_OVER, split_axis=0, concat_axis=0, tiled=True)  47.9 us
    ppermute x2, waiting for transfers between devices, per_device(): parts.append((dq, mine, lax.ppermute(part, 'half', [(1, 0)])))  7.68 us
    ppermute x2, starting transfers between devices, per_device(): firsts = [lax.ppermute(own, 'half', [(0, 1)]) for own in owns]  5.69 us
    pallas_call x2, Pallas kernels, attention(): pl.pallas_call(body, grid=(1,), in_specs=[whole(a.shape) for a in (info,...  5.02 us
    ppermute x2, waiting for transfers between devices, per_device(): firsts = [lax.ppermute(own, 'half', [(0, 1)]) for own in owns]  4.06 us
  transfers between devices with their start and end apart: 4, of which 4 were waited for; matrix products, arithmetic and copies ran while one was open for 1% of the time, Pallas kernels for 4%

profile of v4, /device:TPU:1, one launch (start us, length us, event | category | flops | bytes accessed | tf_op | source)
XLA Modules:
  0.0 137.6 jit_solution(4831296143319208416)
XLA Ops:
  0.6 0.0 copy-start.4
  0.6 0.0 copy-start.1
  0.7 0.0 copy-start
  0.7 1.3 fusion
  2.0 4.4 %collective-permute-start = (bf16[128,1024]{1,0:T(8,128)(2,1)S(1)}, bf16[128,1024]{1,0:T(8,128)(2,1)S(1)}, u32[]{:S(2)}, u32[]{:S(2)}) collective-permute-start(bf16[128,1024]{1,0:T(8,128)(2,1)S(1)} %pad_maximum_fusion.refs_3_), channel_id=1, source_target_pairs={{0,1},{2,3},{4,5},{6,7},{8,9},{10,11},{12,13},{14,15},{16,17},{18,... | collective-permute-start | bytes 786440 | tf_op jit(solution)/shard_map/ppermute | solution.py:197
  6.4 1.3 collective-permute-start.2
  7.7 0.0 copy-done.4
  7.7 0.6 dynamic_slice.3
  8.3 0.6 compare_select_fusion
  9.0 2.3 %collective-permute-done.refs_4_ = bf16[128,1024]{1,0:T(8,128)(2,1)S(1)} collective-permute-done((bf16[128,1024]{1,0:T(8,128)(2,1)S(1)}, bf16[128,1024]{1,0:T(8,128)(2,1)S(1)}, u32[]{:S(2)}, u32[]{:S(2)}) %collective-permute-start) | collective-permute-done | bytes 262176 | tf_op jit(solution)/shard_map/ppermute | solution.py:197
  11.3 0.1 broadcast_in_dim.28.refs_0_
  11.4 0.0 copy-done.1
  11.4 0.0 copy-done
  11.4 2.5 %attention0.1 = (bf16[8,8,16,256]{3,2,1,0:T(8,128)(2,1)S(1)}, f32[8,8,16,128]{3,2,1,0:T(8,128)S(1)}, bf16[8,8,16,128]{3,2,1,0:T(8,128)(2,1)S(1)}) custom-call(s32[16,256]{1,0:T(8,128)S(1)} %broadcast_in_dim.28.refs_0_, bf16[128,4096]{1,0:T(8,128)(2,1)S(1)} %copy-done, bf16[128,4096]{1,0:T(8,128)(2,1)S(1)} %copy-done.1, ...), custom_call_target="tpu_custom_call" | custom-call | tf_op jit(solution)/shard_map/attention0/pallas_call | solution.py:90
  13.9 1.3 collective-permute-start.1
  15.2 1.7 %collective-permute-done.2.refs_4_ = bf16[128,1024]{1,0:T(8,128)(2,1)S(1)} collective-permute-done((bf16[128,1024]{1,0:T(8,128)(2,1)S(1)}, bf16[128,1024]{1,0:T(8,128)(2,1)S(1)}, u32[]{:S(2)}, u32[]{:S(2)}) %collective-permute-start.2) | collective-permute-done | bytes 262176 | tf_op jit(solution)/shard_map/ppermute | solution.py:197
  16.9 2.5 %attention4.1 = (bf16[8,8,16,256]{3,2,1,0:T(8,128)(2,1)S(1)}, f32[8,8,16,128]{3,2,1,0:T(8,128)S(1)}, bf16[8,8,16,128]{3,2,1,0:T(8,128)(2,1)S(1)}) custom-call(s32[16,256]{1,0:T(8,128)S(1)} %broadcast_in_dim.28.refs_0_, bf16[128,4096]{1,0:T(8,128)(2,1)S(1)} %copy-done, bf16[128,4096]{1,0:T(8,128)(2,1)S(1)} %copy-done.1, ...), custom_call_target="tpu_custom_call" | custom-call | tf_op jit(solution)/shard_map/attention4/pallas_call | solution.py:90
  19.4 1.3 collective-permute-start.3
  20.7 0.4 collective-permute-done.1.refs_2_
  21.1 7.3 %collective-permute-done.3.refs_5_ = bf16[8,8,16,128]{3,2,1,0:T(8,128)(2,1)S(1)} collective-permute-done((bf16[8,8,16,128]{3,2,1,0:T(8,128)(2,1)S(1)}, bf16[8,8,16,128]{3,2,1,0:T(8,128)(2,1)S(1)}, u32[]{:S(2)}, u32[]{:S(2)}) %collective-permute-start.3) | collective-permute-done | bytes 262176 | tf_op jit(solution)/shard_map/ppermute | solution.py:202
  28.4 0.2 combine.1
  28.6 0.0 copy-start.2
  28.6 0.0 copy-start.3
  28.6 58.3 %all_to_all.10.y_ref = bf16[128,16,384]{2,1,0:T(8,128)(2,1)S(1)} all-to-all(bf16[128,16,384]{2,1,0:T(8,128)(2,1)S(1)} %bitcast.4), channel_id=1, replica_groups=mesh['dp'=32,'slot'=4,'half'=2] {'dp','slot'}, dimensions={0} | all-to-all | bytes 3145728 | tf_op jit(solution)/shard_map/all_to_all | solution.py:206
  86.9 0.0 copy-done.2
  86.9 0.0 copy-done.3
  86.9 1.3 reorder.1
  88.2 47.9 %all_to_all.11 = bf16[128,16,384]{2,1,0:T(8,128)(2,1)S(1)} all-to-all(bf16[128,16,384]{2,1,0:T(8,128)(2,1)S(1)} %reorder.1), channel_id=1, replica_groups=mesh['dp'=32,'slot'=4,'half'=2] {'dp','slot'}, dimensions={0} | all-to-all | bytes 3145728 | tf_op jit(solution)/shard_map/all_to_all | solution.py:208
  136.1 1.4 %place.1 = (bf16[128,4096]{1,0:T(8,128)(2,1)}, bf16[128,1024]{1,0:T(8,128)(2,1)}, bf16[128,1024]{1,0:T(8,128)(2,1)}) custom-call(bf16[8,16,16,384]{3,2,1,0:T(8,128)(2,1)S(1)} %bitcast.3), custom_call_target="tpu_custom_call" | custom-call | tf_op jit(solution)/shard_map/place/pallas_call | solution.py:165
  (2 shorter events, 0.0 us)
Async XLA Ops:
  0.6 7.1 %copy-start.4 = (s32[128]{0:T(128)S(1)}, s32[128]{0:T(128)}, u32[]{:S(2)}) copy-start(s32[128]{0:T(128)} %param.11) | copy-start | bytes 1540
  0.6 10.7 %copy-start.1 = (bf16[128,4096]{1,0:T(8,128)(2,1)S(1)}, bf16[128,4096]{1,0:T(8,128)(2,1)}, u32[]{:S(2)}) copy-start(bf16[128,4096]{1,0:T(8,128)(2,1)} %refs_2_.3) | copy-start | bytes 3145732
  0.7 10.7 %copy-start = (bf16[128,4096]{1,0:T(8,128)(2,1)S(1)}, bf16[128,4096]{1,0:T(8,128)(2,1)}, u32[]{:S(2)}) copy-start(bf16[128,4096]{1,0:T(8,128)(2,1)} %refs_1_.3) | copy-start | bytes 3145732
  2.0 9.3 %collective-permute-start = (bf16[128,1024]{1,0:T(8,128)(2,1)S(1)}, bf16[128,1024]{1,0:T(8,128)(2,1)S(1)}, u32[]{:S(2)}, u32[]{:S(2)}) collective-permute-start(bf16[128,1024]{1,0:T(8,128)(2,1)S(1)} %pad_maximum_fusion.refs_3_), channel_id=1, source_target_pairs={{0,1},{2,3},{4,5},{6,7},{8,9},{10,11},{12,13},{14,15},{16,17},{18,... | collective-permute-start | bytes 786440 | tf_op jit(solution)/shard_map/ppermute | solution.py:197
  6.4 10.5 %collective-permute-start.2 = (bf16[128,1024]{1,0:T(8,128)(2,1)S(1)}, bf16[128,1024]{1,0:T(8,128)(2,1)S(1)}, u32[]{:S(2)}, u32[]{:S(2)}) collective-permute-start(bf16[128,1024]{1,0:T(8,128)(2,1)S(1)} %pad_maximum_fusion.1.refs_3_), channel_id=1, source_target_pairs={{0,1},{2,3},{4,5},{6,7},{8,9},{10,11},{12,13},{14,15},{16,17},{18,... | collective-permute-start | bytes 786440 | tf_op jit(solution)/shard_map/ppermute | solution.py:197
  13.9 7.2 %collective-permute-start.1 = (bf16[8,8,16,128]{3,2,1,0:T(8,128)(2,1)S(1)}, bf16[8,8,16,128]{3,2,1,0:T(8,128)(2,1)S(1)}, u32[]{:S(2)}, u32[]{:S(2)}) collective-permute-start(bf16[8,8,16,128]{3,2,1,0:T(8,128)(2,1)S(1)} %get-tuple-element.11), channel_id=1, source_target_pairs={{1,0},{3,2},{5,4},{7,6},{9,8},{11,10},{13,12},{15,14},{17,16},{19,... | collective-permute-start | bytes 786440 | tf_op jit(solution)/shard_map/ppermute | solution.py:202
  19.4 9.0 %collective-permute-start.3 = (bf16[8,8,16,128]{3,2,1,0:T(8,128)(2,1)S(1)}, bf16[8,8,16,128]{3,2,1,0:T(8,128)(2,1)S(1)}, u32[]{:S(2)}, u32[]{:S(2)}) collective-permute-start(bf16[8,8,16,128]{3,2,1,0:T(8,128)(2,1)S(1)} %get-tuple-element.14), channel_id=1, source_target_pairs={{1,0},{3,2},{5,4},{7,6},{9,8},{11,10},{13,12},{15,14},{17,16},{19,... | collective-permute-start | bytes 786440 | tf_op jit(solution)/shard_map/ppermute | solution.py:202
  28.6 58.3 %copy-start.2 = (s32[128]{0:T(128)S(1)}, s32[128]{0:T(128)}, u32[]{:S(2)}) copy-start(s32[128]{0:T(128)} %pack_of.1) | copy-start | bytes 1540
  28.6 58.3 %copy-start.3 = (s32[128]{0:T(128)S(1)}, s32[128]{0:T(128)}, u32[]{:S(2)}) copy-start(s32[128]{0:T(128)} %pack_offset.1) | copy-start | bytes 1540

commit v5 on v4

--- a/solution.py
+++ b/solution.py
@@ -12,7 +12,7 @@
 PAIR = 256
 HALF = 128
 GROUP = 4
-CHUNKS = (4, 4)
+CHUNKS = (3, 3, 2)
 VMEM_ATT = 32
 PLACE_STEPS = 2
 TILE = 16
@@ -22,7 +22,21 @@
 CONTRACT_FIRST = (((0,), (0,)), ((), ()))
 
 
-def attention_kernel(lo, hi, info_ref, q_ref, g_ref, own_ref, first_ref, dq_ref, mine_ref, part_ref):
+def four(ref, head):
+    left = head * GROUP * WIDTH
+    return jnp.concatenate([ref[:, left + i * WIDTH : left + (i + 1) * WIDTH] for i in range(GROUP)], axis=0)
+
+
+def both(first_ref, own_ref, block):
+    at = slice(block * WIDTH, (block + 1) * WIDTH)
+    return jnp.concatenate([first_ref[:, at], own_ref[:, at]], axis=0)
+
+
+def tiles(block):
+    return block.reshape(HALF // TILE, TILE, WIDTH)
+
+
+def score_kernel(lo, hi, info_ref, q_ref, g_ref, own_ref, first_ref, probs_ref, dscore_ref, part_ref):
     chosen = info_ref[0:1, :]
     second = info_ref[8:9, :]
     scale = 1.0 / math.sqrt(WIDTH)
@@ -35,67 +49,76 @@
     low = jnp.where(row >= chosen, chosen, 0)
     allowed = (col >= low) & (col <= row)
 
-    def four(ref, h):
-        left = (lo + h) * GROUP * WIDTH
-        return jnp.concatenate([ref[:, left + i * WIDTH : left + (i + 1) * WIDTH] for i in range(GROUP)], axis=0)
-
-    def both(h):
-        at = slice(h * WIDTH, (h + 1) * WIDTH)
-        return jnp.concatenate([first_ref[:, at], own_ref[:, at]], axis=0)
-
-    def tiles(block):
-        return block.reshape(HALF // TILE, TILE, WIDTH)
-
     products = []
     for h in range(heads):
-        scores = lax.dot_general(four(q_ref, h), both(h), CONTRACT_LAST, preferred_element_type=f32)
-        dprob = lax.dot_general(four(g_ref, h), both(heads + h), CONTRACT_LAST, preferred_element_type=f32)
+        keys, values = both(first_ref, own_ref, h), both(first_ref, own_ref, heads + h)
+        scores = lax.dot_general(four(q_ref, lo + h), keys, CONTRACT_LAST, preferred_element_type=f32)
+        dprob = lax.dot_general(four(g_ref, lo + h), values, CONTRACT_LAST, preferred_element_type=f32)
         products.append((scores, dprob))
-    factors = []
-    for scores, dprob in products:
+    for h, (scores, dprob) in enumerate(products):
         scores = jnp.where(allowed[None], scores.reshape(GROUP, HALF, PAIR), -1e30).reshape(GROUP * HALF, PAIR)
         peak = jnp.max(scores, axis=1, keepdims=True)
         weights = jnp.exp2((scores - peak) * (scale * math.log2(math.e)))
         probs = weights * (1.0 / jnp.sum(weights, axis=1, keepdims=True))
         probs_b = probs.astype(bf16)
         delta = jnp.sum(probs_b.astype(f32) * dprob, axis=1, keepdims=True)
-        factors.append((probs_b, (probs * (dprob - delta)).astype(bf16)))
-    for h, (probs_b, dscore_b) in enumerate(factors):
-        dq = jnp.dot(dscore_b, both(h), preferred_element_type=f32) * scale
-        dk = lax.dot_general(dscore_b, four(q_ref, h), CONTRACT_FIRST, preferred_element_type=f32) * scale
-        dv = lax.dot_general(probs_b, four(g_ref, h), CONTRACT_FIRST, preferred_element_type=f32)
+        dscore_b = (probs * (dprob - delta)).astype(bf16)
+        probs_ref[h] = probs_b
+        dscore_ref[h] = dscore_b
+        q4, g4 = four(q_ref, lo + h), four(g_ref, lo + h)
+        dk = lax.dot_general(dscore_b[:, :HALF], q4, CONTRACT_FIRST, preferred_element_type=f32) * scale
+        dv = lax.dot_general(probs_b[:, :HALF], g4, CONTRACT_FIRST, preferred_element_type=f32)
+        part_ref[:, 2 * h] = tiles(dk).astype(bf16)
+        part_ref[:, 2 * h + 1] = tiles(dv).astype(bf16)
+
+
+def gradient_kernel(lo, hi, probs_ref, dscore_ref, q_ref, g_ref, own_ref, first_ref, dq_ref, mine_ref):
+    scale = 1.0 / math.sqrt(WIDTH)
+    f32 = jnp.float32
+    for h in range(hi - lo):
+        dscore_b = dscore_ref[h]
+        dq = jnp.dot(dscore_b, both(first_ref, own_ref, h), preferred_element_type=f32) * scale
         for i in range(GROUP):
             at = slice((i % 2) * WIDTH, (i % 2 + 1) * WIDTH)
-            dq_ref[:, 2 * h + i // 2, :, at] = tiles(dq[i * HALF : (i + 1) * HALF]).astype(bf16)
-        mine_ref[:, 2 * h] = tiles(dk[HALF:])
-        mine_ref[:, 2 * h + 1] = tiles(dv[HALF:])
-        part_ref[:, 2 * h] = tiles(dk[:HALF]).astype(bf16)
-        part_ref[:, 2 * h + 1] = tiles(dv[:HALF]).astype(bf16)
+            dq_ref[:, 2 * h + i // 2, :, at] = tiles(dq[i * HALF : (i + 1) * HALF]).astype(jnp.bfloat16)
+        q4, g4 = four(q_ref, lo + h), four(g_ref, lo + h)
+        dk = lax.dot_general(dscore_b[:, HALF:], q4, CONTRACT_FIRST, preferred_element_type=f32) * scale
+        dv = lax.dot_general(probs_ref[h][:, HALF:], g4, CONTRACT_FIRST, preferred_element_type=f32)
+        mine_ref[:, 2 * h] = tiles(dk)
+        mine_ref[:, 2 * h + 1] = tiles(dv)
 
 
 def whole(shape):
     return pl.BlockSpec(shape, lambda i, *_: (0,) * len(shape))
 
 
-def attention(info, q, g, own, first, lo, hi, before):
-    rows = (HALF // TILE, 2 * (hi - lo), TILE)
-    outs = [
-        jax.ShapeDtypeStruct(rows + (2 * WIDTH,), jnp.bfloat16),
-        jax.ShapeDtypeStruct(rows + (WIDTH,), jnp.float32),
-        jax.ShapeDtypeStruct(rows + (WIDTH,), jnp.bfloat16),
-    ]
+def in_order(kernel, name, operands, before, outs):
     def body(*refs):
-        attention_kernel(lo, hi, *refs[:5], *refs[5 + len(before) :])
+        kernel(*refs[: len(operands)], *refs[len(operands) + len(before) :])
 
     return pl.pallas_call(
         body,
         grid=(1,),
-        in_specs=[whole(a.shape) for a in (info, q, g, own, first)] + [pl.BlockSpec(memory_space=pl.ANY)] * len(before),
+        in_specs=[whole(a.shape) for a in operands] + [pl.BlockSpec(memory_space=pl.ANY)] * len(before),
         out_specs=[whole(a.shape) for a in outs],
         out_shape=outs,
         compiler_params=pltpu.CompilerParams(vmem_limit_bytes=VMEM_ATT * 1024 * 1024),
-        name=f"attention{lo}",
-    )(info, q, g, own, first, *before)
+        name=name,
+    )(*operands, *before)
+
+
+def score(info, q, g, own, first, lo, hi, before):
+    factor = jax.ShapeDtypeStruct((hi - lo, GROUP * HALF, PAIR), jnp.bfloat16)
+    part = jax.ShapeDtypeStruct((HALF // TILE, 2 * (hi - lo), TILE, WIDTH), jnp.bfloat16)
+    kernel = functools.partial(score_kernel, lo, hi)
+    return in_order(kernel, f"score{lo}", (info, q, g, own, first), before, [factor, factor, part])
+
+
+def gradient(probs, dscore, q, g, own, first, lo, hi, before):
+    rows = (HALF // TILE, 2 * (hi - lo), TILE)
+    outs = [jax.ShapeDtypeStruct(rows + (2 * WIDTH,), jnp.bfloat16), jax.ShapeDtypeStruct(rows + (WIDTH,), jnp.float32)]
+    kernel = functools.partial(gradient_kernel, lo, hi)
+    return in_order(kernel, f"gradient{lo}", (probs, dscore, q, g, own, first), before, outs)
 
 
 def combine_kernel(*refs):
@@ -195,11 +218,16 @@
         for lo, hi in cuts
     ]
     firsts = [lax.ppermute(own, "half", [(0, 1)]) for own in owns]
+    factors, last = [], []
+    for (lo, hi), own, first in zip(cuts, owns, firsts):
+        probs, dscore, part = score(info, queries, grad_out, own, first, lo, hi, last)
+        factors.append((probs, dscore, lax.ppermute(part, "half", [(1, 0)])))
+        last = [dscore]
     parts = []
-    for (lo, hi), own, first in zip(cuts, owns, firsts):
-        before = [parts[-1][0]] if parts else []
-        dq, mine, part = attention(info, queries, grad_out, own, first, lo, hi, before)
-        parts.append((dq, mine, lax.ppermute(part, "half", [(1, 0)])))
+    for (lo, hi), own, first, (probs, dscore, part) in zip(cuts, owns, firsts, factors):
+        dq, mine = gradient(probs, dscore, queries, grad_out, own, first, lo, hi, last)
+        parts.append((dq, mine, part))
+        last = [dq]
     pieces = combine(parts, heads)
     shape = pieces.shape
     piece = (pairs,) + shape[2:]

time: 138 us -> 137 us (level)
  waiting for transfers between devices: 11.7 us -> 6.22 us
  starting transfers between devices: 8.28 us -> 10.9 us
  local copies, waits for them, and re-layouts: 1.96 us -> 3.6 us
    ppermute x2 -> x3, waiting for transfers between devices: 4.06 us -> 0.01 us  [per_device(): firsts = [lax.ppermute(own, 'half', [(0, 1)]) for own in owns]]
    ppermute x2 -> x3, waiting for transfers between devices: 7.68 us -> 6.21 us  [per_device(): factors.append((probs, dscore, lax.ppermute(part, 'half', [(1, 0)])))]
    ppermute x2 -> x3, starting transfers between devices: 2.58 us -> 3.88 us  [per_device(): factors.append((probs, dscore, lax.ppermute(part, 'half', [(1, 0)])))]
    ppermute x2 -> x3, starting transfers between devices: 5.69 us -> 6.98 us  [per_device(): firsts = [lax.ppermute(own, 'half', [(0, 1)]) for own in owns]]
    pallas_call x2 -> x6, Pallas kernels: 5.02 us -> 5.96 us  [in_order(): pl.pallas_call(body, grid=(1,), in_specs=[whole(a.shape) for a in operand...]
  transfers between devices with their start and end apart: 4 -> 6, of which waited for: 4 -> 1; matrix products, arithmetic and copies ran while one was open for 1% -> 2% of each run, Pallas kernels for 4% -> 4%
where the time goes in v5:
time: 137 us
  blocking collectives  106 us (77%)
  starting transfers between devices  10.9 us (8%)
  Pallas kernels  8.88 us (6%)
  waiting for transfers between devices  6.22 us (5%)
  local copies, waits for them, and re-layouts  3.6 us (3%)
    all_to_all x1, blocking collectives, per_device(): lax.all_to_all(pieces.reshape(piece), PAIRS_OVER, split_axis=0, concat_ax...  57.9 us
    all_to_all x1, blocking collectives, per_device(): lax.all_to_all(ordered, PAIRS_OVER, split_axis=0, concat_axis=0, tiled=True)  47.9 us
    ppermute x3, starting transfers between devices, per_device(): firsts = [lax.ppermute(own, 'half', [(0, 1)]) for own in owns]  6.98 us
    ppermute x3, waiting for transfers between devices, per_device(): factors.append((probs, dscore, lax.ppermute(part, 'half', [(1, 0)])))  6.21 us
    pallas_call x6, Pallas kernels, in_order(): pl.pallas_call(body, grid=(1,), in_specs=[whole(a.shape) for a in operand...  5.96 us
    ppermute x3, starting transfers between devices, per_device(): factors.append((probs, dscore, lax.ppermute(part, 'half', [(1, 0)])))  3.88 us
  transfers between devices with their start and end apart: 6, of which 1 were waited for; matrix products, arithmetic and copies ran while one was open for 2% of the time, Pallas kernels for 4%

profile of v5, /device:TPU:1, one launch (start us, length us, event | category | flops | bytes accessed | tf_op | source)
XLA Modules:
  0.0 136.9 jit_solution(12079730183180822058)
XLA Ops:
  0.6 0.0 copy-start.4
  0.6 0.0 copy-start.1
  0.7 0.0 copy-start
  0.7 1.2 fusion
  1.9 4.4 %collective-permute-start = (bf16[128,768]{1,0:T(8,128)(2,1)S(1)}, bf16[128,768]{1,0:T(8,128)(2,1)S(1)}, u32[]{:S(2)}, u32[]{:S(2)}) collective-permute-start(bf16[128,768]{1,0:T(8,128)(2,1)S(1)} %pad_maximum_fusion.refs_3_.refs_4_), channel_id=1, source_target_pairs={{0,1},{2,3},{4,5},{6,7},{8,9},{10,11},{12,13},{14,15},{16,17},{18,... | collective-permute-start | bytes 589832 | tf_op jit(solution)/shard_map/ppermute | solution.py:220
  6.3 1.3 collective-permute-start.2
  7.6 0.8 slice.20
  8.5 0.8 slice.21
  9.4 1.3 collective-permute-start.1
  10.7 0.0 copy-done.4
  10.7 0.6 dynamic_slice.3
  11.3 0.6 compare_select_fusion
  11.9 0.0 collective-permute-done.refs_4_.refs_5_
  11.9 0.1 broadcast_in_dim.28.refs_0_
  12.0 0.0 copy-done.1
  12.0 0.0 copy-done
  12.0 1.5 %score0.1 = (bf16[3,512,256]{2,1,0:T(8,128)(2,1)S(1)}, bf16[3,512,256]{2,1,0:T(8,128)(2,1)S(1)}, bf16[8,6,16,128]{3,2,1,0:T(8,128)(2,1)S(1)}) custom-call(s32[16,256]{1,0:T(8,128)S(1)} %broadcast_in_dim.28.refs_0_, bf16[128,4096]{1,0:T(8,128)(2,1)S(1)} %copy-done, bf16[128,4096]{1,0:T(8,128)(2,1)S(1)} %copy-done.1, ...), custom_call_target="tpu_custom_call" | custom-call | tf_op jit(solution)/shard_map/score0/pallas_call | solution.py:99
  13.6 1.3 collective-permute-start.3
  14.9 0.0 collective-permute-done.2.refs_4_.refs_5_
  14.9 1.6 %score3.1 = (bf16[3,512,256]{2,1,0:T(8,128)(2,1)S(1)}, bf16[3,512,256]{2,1,0:T(8,128)(2,1)S(1)}, bf16[8,6,16,128]{3,2,1,0:T(8,128)(2,1)S(1)}) custom-call(s32[16,256]{1,0:T(8,128)S(1)} %broadcast_in_dim.28.refs_0_, bf16[128,4096]{1,0:T(8,128)(2,1)S(1)} %copy-done, bf16[128,4096]{1,0:T(8,128)(2,1)S(1)} %copy-done.1, ...), custom_call_target="tpu_custom_call" | custom-call | tf_op jit(solution)/shard_map/score3/pallas_call | solution.py:99
  16.4 1.3 collective-permute-start.4
  17.7 0.0 collective-permute-done.1.refs_4_.refs_5_
  17.7 1.2 score6.1
  18.9 1.3 collective-permute-start.5
  20.2 0.6 gradient0.1
  20.8 0.6 gradient3.1
  21.4 0.5 gradient6.1
  21.9 6.2 %collective-permute-done.5.refs_8_ = bf16[8,4,16,128]{3,2,1,0:T(8,128)(2,1)S(1)} collective-permute-done((bf16[8,4,16,128]{3,2,1,0:T(8,128)(2,1)S(1)}, bf16[8,4,16,128]{3,2,1,0:T(8,128)(2,1)S(1)}, u32[]{:S(2)}, u32[]{:S(2)}) %collective-permute-start.5) | collective-permute-done | bytes 131104 | tf_op jit(solution)/shard_map/ppermute | solution.py:224
  28.1 0.0 collective-permute-done.3.refs_2_
  28.1 0.0 collective-permute-done.4.refs_5_
  28.1 0.2 combine.1
  28.3 0.0 copy-start.2
  28.3 0.0 copy-start.3
  28.3 57.9 %all_to_all.10.y_ref = bf16[128,16,384]{2,1,0:T(8,128)(2,1)S(1)} all-to-all(bf16[128,16,384]{2,1,0:T(8,128)(2,1)S(1)} %bitcast.4), channel_id=1, replica_groups=mesh['dp'=32,'slot'=4,'half'=2] {'dp','slot'}, dimensions={0} | all-to-all | bytes 3145728 | tf_op jit(solution)/shard_map/all_to_all | solution.py:234
  86.2 0.0 copy-done.2
  86.2 0.0 copy-done.3
  86.2 1.3 reorder.1
  87.6 47.9 %all_to_all.11 = bf16[128,16,384]{2,1,0:T(8,128)(2,1)S(1)} all-to-all(bf16[128,16,384]{2,1,0:T(8,128)(2,1)S(1)} %reorder.1), channel_id=1, replica_groups=mesh['dp'=32,'slot'=4,'half'=2] {'dp','slot'}, dimensions={0} | all-to-all | bytes 3145728 | tf_op jit(solution)/shard_map/all_to_all | solution.py:236
  135.5 1.4 %place.1 = (bf16[128,4096]{1,0:T(8,128)(2,1)}, bf16[128,1024]{1,0:T(8,128)(2,1)}, bf16[128,1024]{1,0:T(8,128)(2,1)}) custom-call(bf16[8,16,16,384]{3,2,1,0:T(8,128)(2,1)S(1)} %bitcast.3), custom_call_target="tpu_custom_call" | custom-call | tf_op jit(solution)/shard_map/place/pallas_call | solution.py:188
  (3 shorter events, 0.0 us)
Async XLA Ops:
  0.6 10.0 %copy-start.4 = (s32[128]{0:T(128)S(1)}, s32[128]{0:T(128)}, u32[]{:S(2)}) copy-start(s32[128]{0:T(128)} %param.11) | copy-start | bytes 1540
  0.6 11.4 %copy-start.1 = (bf16[128,4096]{1,0:T(8,128)(2,1)S(1)}, bf16[128,4096]{1,0:T(8,128)(2,1)}, u32[]{:S(2)}) copy-start(bf16[128,4096]{1,0:T(8,128)(2,1)} %refs_3_.5) | copy-start | bytes 3145732
  0.7 11.4 %copy-start = (bf16[128,4096]{1,0:T(8,128)(2,1)S(1)}, bf16[128,4096]{1,0:T(8,128)(2,1)}, u32[]{:S(2)}) copy-start(bf16[128,4096]{1,0:T(8,128)(2,1)} %refs_2_.11) | copy-start | bytes 3145732
  1.9 10.0 %collective-permute-start = (bf16[128,768]{1,0:T(8,128)(2,1)S(1)}, bf16[128,768]{1,0:T(8,128)(2,1)S(1)}, u32[]{:S(2)}, u32[]{:S(2)}) collective-permute-start(bf16[128,768]{1,0:T(8,128)(2,1)S(1)} %pad_maximum_fusion.refs_3_.refs_4_), channel_id=1, source_target_pairs={{0,1},{2,3},{4,5},{6,7},{8,9},{10,11},{12,13},{14,15},{16,17},{18,... | collective-permute-start | bytes 589832 | tf_op jit(solution)/shard_map/ppermute | solution.py:220
  6.3 8.5 %collective-permute-start.2 = (bf16[128,768]{1,0:T(8,128)(2,1)S(1)}, bf16[128,768]{1,0:T(8,128)(2,1)S(1)}, u32[]{:S(2)}, u32[]{:S(2)}) collective-permute-start(bf16[128,768]{1,0:T(8,128)(2,1)S(1)} %pad_maximum_fusion.1.refs_3_.refs_4_), channel_id=1, source_target_pairs={{0,1},{2,3},{4,5},{6,7},{8,9},{10,11},{12,13},{14,15},{16,17},{18,... | collective-permute-start | bytes 589832 | tf_op jit(solution)/shard_map/ppermute | solution.py:220
  9.4 8.4 %collective-permute-start.1 = (bf16[128,512]{1,0:T(8,128)(2,1)S(1)}, bf16[128,512]{1,0:T(8,128)(2,1)S(1)}, u32[]{:S(2)}, u32[]{:S(2)}) collective-permute-start(bf16[128,512]{1,0:T(8,128)(2,1)S(1)} %pad_maximum_fusion.2.refs_3_.refs_4_), channel_id=1, source_target_pairs={{0,1},{2,3},{4,5},{6,7},{8,9},{10,11},{12,13},{14,15},{16,17},{18,... | collective-permute-start | bytes 393224 | tf_op jit(solution)/shard_map/ppermute | solution.py:220
  13.6 14.6 %collective-permute-start.3 = (bf16[8,6,16,128]{3,2,1,0:T(8,128)(2,1)S(1)}, bf16[8,6,16,128]{3,2,1,0:T(8,128)(2,1)S(1)}, u32[]{:S(2)}, u32[]{:S(2)}) collective-permute-start(bf16[8,6,16,128]{3,2,1,0:T(8,128)(2,1)S(1)} %get-tuple-element.24), channel_id=1, source_target_pairs={{1,0},{3,2},{5,4},{7,6},{9,8},{11,10},{13,12},{15,14},{17,16},{19,... | collective-permute-start | bytes 589832 | tf_op jit(solution)/shard_map/ppermute | solution.py:224
  16.4 11.7 %collective-permute-start.4 = (bf16[8,6,16,128]{3,2,1,0:T(8,128)(2,1)S(1)}, bf16[8,6,16,128]{3,2,1,0:T(8,128)(2,1)S(1)}, u32[]{:S(2)}, u32[]{:S(2)}) collective-permute-start(bf16[8,6,16,128]{3,2,1,0:T(8,128)(2,1)S(1)} %get-tuple-element.28), channel_id=1, source_target_pairs={{1,0},{3,2},{5,4},{7,6},{9,8},{11,10},{13,12},{15,14},{17,16},{19,... | collective-permute-start | bytes 589832 | tf_op jit(solution)/shard_map/ppermute | solution.py:224
  18.9 9.2 %collective-permute-start.5 = (bf16[8,4,16,128]{3,2,1,0:T(8,128)(2,1)S(1)}, bf16[8,4,16,128]{3,2,1,0:T(8,128)(2,1)S(1)}, u32[]{:S(2)}, u32[]{:S(2)}) collective-permute-start(bf16[8,4,16,128]{3,2,1,0:T(8,128)(2,1)S(1)} %get-tuple-element.32), channel_id=1, source_target_pairs={{1,0},{3,2},{5,4},{7,6},{9,8},{11,10},{13,12},{15,14},{17,16},{19,... | collective-permute-start | bytes 393224 | tf_op jit(solution)/shard_map/ppermute | solution.py:224
  28.3 57.9 %copy-start.2 = (s32[128]{0:T(128)S(1)}, s32[128]{0:T(128)}, u32[]{:S(2)}) copy-start(s32[128]{0:T(128)} %pack_of.1) | copy-start | bytes 1540
  28.3 57.9 %copy-start.3 = (s32[128]{0:T(128)S(1)}, s32[128]{0:T(128)}, u32[]{:S(2)}) copy-start(s32[128]{0:T(128)} %pack_offset.1) | copy-start | bytes 1540

commit v6 on v5

--- a/solution.py
+++ b/solution.py
@@ -14,7 +14,7 @@
 GROUP = 4
 CHUNKS = (3, 3, 2)
 VMEM_ATT = 32
-PLACE_STEPS = 2
+PLACE_STEPS = 1
 TILE = 16
 PAIRS_OVER = ("dp", "slot")
 ALL = ("dp", "slot", "half")

time: 137 us -> 137 us (level)
  no operation moved by 1% of the time
where the time goes in v6:
time: 137 us
  blocking collectives  106 us (77%)
  starting transfers between devices  10.9 us (8%)
  Pallas kernels  8.85 us (6%)
  waiting for transfers between devices  6.22 us (5%)
  local copies, waits for them, and re-layouts  3.6 us (3%)
    all_to_all x1, blocking collectives, per_device(): lax.all_to_all(pieces.reshape(piece), PAIRS_OVER, split_axis=0, concat_ax...  57.9 us
    all_to_all x1, blocking collectives, per_device(): lax.all_to_all(ordered, PAIRS_OVER, split_axis=0, concat_axis=0, tiled=True)  47.9 us
    ppermute x3, starting transfers between devices, per_device(): firsts = [lax.ppermute(own, 'half', [(0, 1)]) for own in owns]  6.98 us
    ppermute x3, waiting for transfers between devices, per_device(): factors.append((probs, dscore, lax.ppermute(part, 'half', [(1, 0)])))  6.21 us
    pallas_call x6, Pallas kernels, in_order(): pl.pallas_call(body, grid=(1,), in_specs=[whole(a.shape) for a in operand...  5.96 us
    ppermute x3, starting transfers between devices, per_device(): factors.append((probs, dscore, lax.ppermute(part, 'half', [(1, 0)])))  3.88 us
  transfers between devices with their start and end apart: 6, of which 1 were waited for; matrix products, arithmetic and copies ran while one was open for 2% of the time, Pallas kernels for 4%

profile of v6, /device:TPU:1, one launch (start us, length us, event | category | flops | bytes accessed | tf_op | source)
XLA Modules:
  0.0 136.9 jit_solution(17210762243580905098)
XLA Ops:
  0.6 0.0 copy-start.4
  0.6 0.0 copy-start.1
  0.7 0.0 copy-start
  0.7 1.2 fusion
  1.9 4.4 %collective-permute-start = (bf16[128,768]{1,0:T(8,128)(2,1)S(1)}, bf16[128,768]{1,0:T(8,128)(2,1)S(1)}, u32[]{:S(2)}, u32[]{:S(2)}) collective-permute-start(bf16[128,768]{1,0:T(8,128)(2,1)S(1)} %pad_maximum_fusion.refs_3_.refs_4_), channel_id=1, source_target_pairs={{0,1},{2,3},{4,5},{6,7},{8,9},{10,11},{12,13},{14,15},{16,17},{18,... | collective-permute-start | bytes 589832 | tf_op jit(solution)/shard_map/ppermute | solution.py:220
  6.3 1.3 collective-permute-start.2
  7.6 0.8 slice.20
  8.5 0.8 slice.21
  9.4 1.3 collective-permute-start.1
  10.7 0.0 copy-done.4
  10.7 0.6 dynamic_slice.3
  11.3 0.6 compare_select_fusion
  11.9 0.0 collective-permute-done.refs_4_.refs_5_
  11.9 0.1 broadcast_in_dim.28.refs_0_
  12.0 0.0 copy-done.1
  12.0 0.0 copy-done
  12.0 1.5 %score0.1 = (bf16[3,512,256]{2,1,0:T(8,128)(2,1)S(1)}, bf16[3,512,256]{2,1,0:T(8,128)(2,1)S(1)}, bf16[8,6,16,128]{3,2,1,0:T(8,128)(2,1)S(1)}) custom-call(s32[16,256]{1,0:T(8,128)S(1)} %broadcast_in_dim.28.refs_0_, bf16[128,4096]{1,0:T(8,128)(2,1)S(1)} %copy-done, bf16[128,4096]{1,0:T(8,128)(2,1)S(1)} %copy-done.1, ...), custom_call_target="tpu_custom_call" | custom-call | tf_op jit(solution)/shard_map/score0/pallas_call | solution.py:99
  13.6 1.3 collective-permute-start.3
  14.9 0.0 collective-permute-done.2.refs_4_.refs_5_
  14.9 1.6 %score3.1 = (bf16[3,512,256]{2,1,0:T(8,128)(2,1)S(1)}, bf16[3,512,256]{2,1,0:T(8,128)(2,1)S(1)}, bf16[8,6,16,128]{3,2,1,0:T(8,128)(2,1)S(1)}) custom-call(s32[16,256]{1,0:T(8,128)S(1)} %broadcast_in_dim.28.refs_0_, bf16[128,4096]{1,0:T(8,128)(2,1)S(1)} %copy-done, bf16[128,4096]{1,0:T(8,128)(2,1)S(1)} %copy-done.1, ...), custom_call_target="tpu_custom_call" | custom-call | tf_op jit(solution)/shard_map/score3/pallas_call | solution.py:99
  16.4 1.3 collective-permute-start.4
  17.7 0.0 collective-permute-done.1.refs_4_.refs_5_
  17.7 1.2 score6.1
  18.9 1.3 collective-permute-start.5
  20.2 0.6 gradient0.1
  20.8 0.6 gradient3.1
  21.4 0.5 gradient6.1
  21.9 6.2 %collective-permute-done.5.refs_8_ = bf16[8,4,16,128]{3,2,1,0:T(8,128)(2,1)S(1)} collective-permute-done((bf16[8,4,16,128]{3,2,1,0:T(8,128)(2,1)S(1)}, bf16[8,4,16,128]{3,2,1,0:T(8,128)(2,1)S(1)}, u32[]{:S(2)}, u32[]{:S(2)}) %collective-permute-start.5) | collective-permute-done | bytes 131104 | tf_op jit(solution)/shard_map/ppermute | solution.py:224
  28.1 0.0 collective-permute-done.3.refs_2_
  28.1 0.0 collective-permute-done.4.refs_5_
  28.1 0.2 combine.1
  28.3 0.0 copy-start.2
  28.3 0.0 copy-start.3
  28.3 57.9 %all_to_all.10.y_ref = bf16[128,16,384]{2,1,0:T(8,128)(2,1)S(1)} all-to-all(bf16[128,16,384]{2,1,0:T(8,128)(2,1)S(1)} %bitcast.4), channel_id=1, replica_groups=mesh['dp'=32,'slot'=4,'half'=2] {'dp','slot'}, dimensions={0} | all-to-all | bytes 3145728 | tf_op jit(solution)/shard_map/all_to_all | solution.py:234
  86.2 0.0 copy-done.2
  86.2 0.0 copy-done.3
  86.2 1.3 reorder.1
  87.6 47.9 %all_to_all.11 = bf16[128,16,384]{2,1,0:T(8,128)(2,1)S(1)} all-to-all(bf16[128,16,384]{2,1,0:T(8,128)(2,1)S(1)} %reorder.1), channel_id=1, replica_groups=mesh['dp'=32,'slot'=4,'half'=2] {'dp','slot'}, dimensions={0} | all-to-all | bytes 3145728 | tf_op jit(solution)/shard_map/all_to_all | solution.py:236
  135.5 1.4 %place.1 = (bf16[128,4096]{1,0:T(8,128)(2,1)}, bf16[128,1024]{1,0:T(8,128)(2,1)}, bf16[128,1024]{1,0:T(8,128)(2,1)}) custom-call(bf16[8,16,16,384]{3,2,1,0:T(8,128)(2,1)S(1)} %bitcast.3), custom_call_target="tpu_custom_call" | custom-call | tf_op jit(solution)/shard_map/place/pallas_call | solution.py:188
  (3 shorter events, 0.0 us)
Async XLA Ops:
  0.6 10.0 %copy-start.4 = (s32[128]{0:T(128)S(1)}, s32[128]{0:T(128)}, u32[]{:S(2)}) copy-start(s32[128]{0:T(128)} %param.11) | copy-start | bytes 1540
  0.6 11.4 %copy-start.1 = (bf16[128,4096]{1,0:T(8,128)(2,1)S(1)}, bf16[128,4096]{1,0:T(8,128)(2,1)}, u32[]{:S(2)}) copy-start(bf16[128,4096]{1,0:T(8,128)(2,1)} %refs_3_.5) | copy-start | bytes 3145732
  0.7 11.4 %copy-start = (bf16[128,4096]{1,0:T(8,128)(2,1)S(1)}, bf16[128,4096]{1,0:T(8,128)(2,1)}, u32[]{:S(2)}) copy-start(bf16[128,4096]{1,0:T(8,128)(2,1)} %refs_2_.11) | copy-start | bytes 3145732
  1.9 10.0 %collective-permute-start = (bf16[128,768]{1,0:T(8,128)(2,1)S(1)}, bf16[128,768]{1,0:T(8,128)(2,1)S(1)}, u32[]{:S(2)}, u32[]{:S(2)}) collective-permute-start(bf16[128,768]{1,0:T(8,128)(2,1)S(1)} %pad_maximum_fusion.refs_3_.refs_4_), channel_id=1, source_target_pairs={{0,1},{2,3},{4,5},{6,7},{8,9},{10,11},{12,13},{14,15},{16,17},{18,... | collective-permute-start | bytes 589832 | tf_op jit(solution)/shard_map/ppermute | solution.py:220
  6.3 8.5 %collective-permute-start.2 = (bf16[128,768]{1,0:T(8,128)(2,1)S(1)}, bf16[128,768]{1,0:T(8,128)(2,1)S(1)}, u32[]{:S(2)}, u32[]{:S(2)}) collective-permute-start(bf16[128,768]{1,0:T(8,128)(2,1)S(1)} %pad_maximum_fusion.1.refs_3_.refs_4_), channel_id=1, source_target_pairs={{0,1},{2,3},{4,5},{6,7},{8,9},{10,11},{12,13},{14,15},{16,17},{18,... | collective-permute-start | bytes 589832 | tf_op jit(solution)/shard_map/ppermute | solution.py:220
  9.4 8.4 %collective-permute-start.1 = (bf16[128,512]{1,0:T(8,128)(2,1)S(1)}, bf16[128,512]{1,0:T(8,128)(2,1)S(1)}, u32[]{:S(2)}, u32[]{:S(2)}) collective-permute-start(bf16[128,512]{1,0:T(8,128)(2,1)S(1)} %pad_maximum_fusion.2.refs_3_.refs_4_), channel_id=1, source_target_pairs={{0,1},{2,3},{4,5},{6,7},{8,9},{10,11},{12,13},{14,15},{16,17},{18,... | collective-permute-start | bytes 393224 | tf_op jit(solution)/shard_map/ppermute | solution.py:220
  13.6 14.6 %collective-permute-start.3 = (bf16[8,6,16,128]{3,2,1,0:T(8,128)(2,1)S(1)}, bf16[8,6,16,128]{3,2,1,0:T(8,128)(2,1)S(1)}, u32[]{:S(2)}, u32[]{:S(2)}) collective-permute-start(bf16[8,6,16,128]{3,2,1,0:T(8,128)(2,1)S(1)} %get-tuple-element.24), channel_id=1, source_target_pairs={{1,0},{3,2},{5,4},{7,6},{9,8},{11,10},{13,12},{15,14},{17,16},{19,... | collective-permute-start | bytes 589832 | tf_op jit(solution)/shard_map/ppermute | solution.py:224
  16.4 11.7 %collective-permute-start.4 = (bf16[8,6,16,128]{3,2,1,0:T(8,128)(2,1)S(1)}, bf16[8,6,16,128]{3,2,1,0:T(8,128)(2,1)S(1)}, u32[]{:S(2)}, u32[]{:S(2)}) collective-permute-start(bf16[8,6,16,128]{3,2,1,0:T(8,128)(2,1)S(1)} %get-tuple-element.28), channel_id=1, source_target_pairs={{1,0},{3,2},{5,4},{7,6},{9,8},{11,10},{13,12},{15,14},{17,16},{19,... | collective-permute-start | bytes 589832 | tf_op jit(solution)/shard_map/ppermute | solution.py:224
  18.9 9.2 %collective-permute-start.5 = (bf16[8,4,16,128]{3,2,1,0:T(8,128)(2,1)S(1)}, bf16[8,4,16,128]{3,2,1,0:T(8,128)(2,1)S(1)}, u32[]{:S(2)}, u32[]{:S(2)}) collective-permute-start(bf16[8,4,16,128]{3,2,1,0:T(8,128)(2,1)S(1)} %get-tuple-element.32), channel_id=1, source_target_pairs={{1,0},{3,2},{5,4},{7,6},{9,8},{11,10},{13,12},{15,14},{17,16},{19,... | collective-permute-start | bytes 393224 | tf_op jit(solution)/shard_map/ppermute | solution.py:224
  28.3 57.9 %copy-start.2 = (s32[128]{0:T(128)S(1)}, s32[128]{0:T(128)}, u32[]{:S(2)}) copy-start(s32[128]{0:T(128)} %pack_of.1) | copy-start | bytes 1540
  28.3 57.9 %copy-start.3 = (s32[128]{0:T(128)S(1)}, s32[128]{0:T(128)}, u32[]{:S(2)}) copy-start(s32[128]{0:T(128)} %pack_offset.1) | copy-start | bytes 1540
